TPU v7x, 32 devices: a whole 2x2x4 slice. The times are simulated.
32 devices in a mesh: leaf: 16 (over z, y, x), rhs: 2 (over core).
Axes of the slice: x: 2, y: 2, z: 4, core: 2. Of those that a mesh axis runs over, the one named last changes fastest.
Arguments:
- points: bfloat16 [2048, 8, 256], P('leaf'), may hold values from -5 to 5
- values: bfloat16 [2048, 16, 256], P('leaf', 'rhs'), parts along dimension 1, may hold values from -6 to 6
- counts: int32 [2048], P('leaf'), may hold values from 128 to 256
- leaf_basis: bfloat16 [2048, 64, 256], P('leaf'), may hold values from -0.375 to 0.375
- transfer: bfloat16 [2048, 64, 64], P('leaf'), may hold values from -0.5 to 0.5
- leaf_skeleton: bfloat16 [2048, 8, 64], P('leaf'), may hold values from -5 to 5
- upper_skeleton: bfloat16 [1024, 8, 64], P('leaf'), may hold values from -5 to 5
- near_list: int32 [2048, 6], P('leaf'), may hold values from 0 to 2047, as said below
- far_owner: int32 [2048, 8], P('leaf'), may hold values from 0 to 15, all different within a row; in each aligned block of 128 rows (0 to 127, 128 to 255, ...) at most 128 rows name the same one
- far_local: int32 [2048, 8], P('leaf'), may hold values from 0 to 127
- upper_owner: int32 [1024, 8], P('leaf'), may hold values from 0 to 15, all different within a row; in each aligned block of 64 rows (0 to 63, 64 to 127, ...) at most 64 rows name the same one
- upper_local: int32 [1024, 8], P('leaf'), may hold values from 0 to 63
Outputs:
- product: float32 [2048, 16, 256], P('leaf', 'rhs'), parts along dimension 1
There are 2 independent parts, one for each index of `rhs`. A program takes and returns all parts, laid end to end along the dimension named above; an argument that names none is the same for every part. Nothing has to cross between parts.
Inputs may be any that keep to these rules, and one draw needn't show every extreme that they name: `near_list`: entry 0 of leaf l's list is l itself; every entry lies within 4 leaves of the block of 128 leaves that holds l, and some lists reach both ends of that range where the grid of leaves allows. `far_owner`: A row's 8 owners are different; among the rows of one device (aligned blocks of 128 rows) no owner is named by more than 128 entries, and some owner by exactly that many. `upper_owner`: A row's 8 owners are different; among the rows of one device (aligned blocks of 64 rows) no owner is named by more than 64 entries, and some owner by exactly that many.
All inputs are finite; a program needn't handle non-finite values.
Results may differ from a plain program's by a relative error of at most 0.0032.
Values may be sent and summed in bfloat16 or wider, within the bound.
A program may use at most 128 MiB of HBM per device.

v0:
```python
import math

import jax
import jax.numpy as jnp
from jax import lax
from jax.sharding import PartitionSpec as P

DIM = 8
HALO = 4


SQRT_THREE = 1.7320508075688772
LENGTH_SCALE = 1.5


def with_halo(cells, sides, width):
    for axis, dim in sides:
        count = lax.axis_size(axis)
        ends = count - 1
        head = lax.slice_in_dim(cells, 0, width, axis=dim)
        tail = lax.slice_in_dim(cells, cells.shape[dim] - width, cells.shape[dim], axis=dim)
        cells = jnp.concatenate(
            [
                lax.ppermute(tail, axis, [(i, (i + 1) % count) for i in range(ends)]),
                cells,
                lax.ppermute(head, axis, [((i + 1) % count, i) for i in range(ends)]),
            ],
            axis=dim,
        )
    return cells


def matern(targets, sources):
    square = 0.0
    for coord in range(targets.shape[-2]):
        offset = targets[..., coord, :, None] - sources[..., coord, None, :]
        square = square + offset * offset
    scaled = SQRT_THREE / LENGTH_SCALE * jnp.sqrt(square)
    return (1.0 + scaled) * jnp.exp(-scaled)


def far_sum(target_skel, source_skel, source_coef):
    kernel = matern(
        target_skel.astype(jnp.float32)[:, None], source_skel.astype(jnp.float32)
    ).astype(jnp.bfloat16)
    return jnp.einsum("nfcb,nfab->nca", source_coef, kernel, preferred_element_type=jnp.float32)


def slot_table(owner, local, owners, capacity):
    flat_owner = owner.reshape(-1)
    flat_local = local.reshape(-1)
    owner_hits = (flat_owner[:, None] == jnp.arange(owners, dtype=jnp.int32)[None, :]).astype(
        jnp.int32
    )
    before = jnp.cumsum(owner_hits, axis=0) - owner_hits
    slot_index = jnp.sum(before * owner_hits, axis=1)
    wanted = jnp.zeros((owners, capacity), jnp.int32).at[flat_owner, slot_index].set(flat_local)
    return (wanted, flat_owner, slot_index)


def body(
    points,
    values,
    counts,
    leaf_basis,
    transfer,
    leaf_skeleton,
    upper_skeleton,
    near_list,
    far_owner,
    far_local,
    upper_owner,
    upper_local,
):
    leaf_dev = points.shape[0]
    leaf_size = points.shape[2]
    columns = values.shape[1]
    rank = leaf_basis.shape[1]
    far_count = far_owner.shape[1]
    par_dev = leaf_dev // 2
    owners = lax.axis_size("leaf")
    point_live = lax.broadcasted_iota(jnp.int32, (leaf_dev, leaf_size), 1) < counts[:, None]
    masked = jnp.where(point_live[:, None, :], values, jnp.zeros_like(values))
    leaf_coef = jnp.einsum(
        "lcp,lkp->lck", masked, leaf_basis, preferred_element_type=jnp.float32
    ).astype(jnp.bfloat16)
    child_coef = leaf_coef.reshape(par_dev, 2, columns, rank)
    child_transfer = transfer.reshape(par_dev, 2, rank, rank)
    upper_coef = jnp.einsum(
        "pjck,pjkm->pcm", child_coef, child_transfer, preferred_element_type=jnp.float32
    ).astype(jnp.bfloat16)
    bundle = jnp.concatenate([points, masked], axis=1)
    extended = with_halo(bundle, (("leaf", 0),), HALO)
    first_leaf = lax.axis_index("leaf") * leaf_dev - HALO
    near_count = near_list.shape[1]
    group_size = math.gcd(leaf_dev, 8)
    turns = leaf_dev // group_size
    local_ids = (near_list - first_leaf).reshape(turns, group_size, near_count)

    def near_block(pieces):
        target_points, chosen = pieces
        source_rows = extended[chosen]
        kernel = matern(
            target_points.astype(jnp.float32)[:, None], source_rows[:, :, :DIM].astype(jnp.float32)
        ).astype(jnp.bfloat16)
        return jnp.einsum(
            "gjcs,gjts->gct", source_rows[:, :, DIM:], kernel, preferred_element_type=jnp.float32
        )

    near_part = lax.map(near_block, (points.reshape(turns, group_size, DIM, leaf_size), local_ids))
    near_part = near_part.reshape(leaf_dev, columns, leaf_size)
    leaf_rows = leaf_coef.reshape(leaf_dev, columns * rank)
    leaf_skel_rows = leaf_skeleton.reshape(leaf_dev, DIM * rank)
    capacity = max(2, 2 * leaf_dev * far_count // owners)
    wanted, flat_owner, slot_index = slot_table(far_owner, far_local, owners, capacity)
    asked = lax.all_to_all(wanted, "leaf", split_axis=0, concat_axis=0, tiled=True)
    got_coef = lax.all_to_all(leaf_rows[asked], "leaf", split_axis=0, concat_axis=0, tiled=True)
    got_skel = lax.all_to_all(
        leaf_skel_rows[asked], "leaf", split_axis=0, concat_axis=0, tiled=True
    )
    picked_coef = got_coef[flat_owner, slot_index]
    picked_skel = got_skel[flat_owner, slot_index]
    leaf_far = far_sum(
        leaf_skeleton,
        picked_skel.reshape(leaf_dev, far_count, DIM, rank),
        picked_coef.reshape(leaf_dev, far_count, columns, rank),
    )
    upper_rows = upper_coef.reshape(par_dev, columns * rank)
    upper_skel_rows = upper_skeleton.reshape(par_dev, DIM * rank)
    upper_capacity = max(2, 2 * par_dev * far_count // owners)
    upper_wanted, upper_flat, upper_slot = slot_table(
        upper_owner, upper_local, owners, upper_capacity
    )
    asked = lax.all_to_all(upper_wanted, "leaf", split_axis=0, concat_axis=0, tiled=True)
    got_upper = lax.all_to_all(upper_rows[asked], "leaf", split_axis=0, concat_axis=0, tiled=True)
    got_upper_skel = lax.all_to_all(
        upper_skel_rows[asked], "leaf", split_axis=0, concat_axis=0, tiled=True
    )
    chosen_coef = got_upper[upper_flat, upper_slot]
    chosen_skel = got_upper_skel[upper_flat, upper_slot]
    upper_field = far_sum(
        upper_skeleton,
        chosen_skel.reshape(par_dev, far_count, DIM, rank),
        chosen_coef.reshape(par_dev, far_count, columns, rank),
    ).astype(jnp.bfloat16)
    spread = jnp.repeat(upper_field, 2, axis=0)
    leaf_field = (
        leaf_far + jnp.einsum("lcm,lkm->lck", spread, transfer, preferred_element_type=jnp.float32)
    ).astype(jnp.bfloat16)
    far_part = jnp.einsum(
        "lck,lkp->lcp", leaf_field, leaf_basis, preferred_element_type=jnp.float32
    )
    return jnp.where(point_live[:, None, :], far_part + near_part, 0.0)


def solution(mesh):
    return jax.shard_map(
        body,
        mesh=mesh,
        in_specs=(
            P("leaf", None, None),
            P("leaf", "rhs", None),
            P("leaf"),
            P("leaf", None, None),
            P("leaf", None, None),
            P("leaf", None, None),
            P("leaf", None, None),
            P("leaf", None),
            P("leaf", None),
            P("leaf", None),
            P("leaf", None),
            P("leaf", None),
        ),
        out_specs=P("leaf", "rhs", None),
        check_vma=False,
    )
```

profile of v0, /device:TPU:0, one launch (start us, length us, event | category | flops | bytes accessed | tf_op | source)
XLA Modules:
  0.0 652.5 jit_solution(6892663241627943206)
XLA Ops:
  4.7 69.6 %scatter_fusion = s32[16,64]{1,0:T(8,128)} fusion(s32[16,64]{1,0:T(8,128)} %broadcast.187, s32[512]{0:T(512)S(1)} %bitcast.215, s32[512]{0:T(512)S(1)} %reshape.403), kind=kCustom, calls=%fused_computation.9 | custom fusion | bytes 10240 | tf_op jit(solution)/shard_map/scatter | solution.py:57
  74.3 8.4 %all-to-all-start.3 = ((s32[16,1,64]{2,1,0:T(1,128)}), s32[16,1,64]{2,1,0:T(1,128)S(1)}, u32[]{:S(2)}, u32[]{:S(2)}) async-start(s32[16,1,64]{2,1,0:T(1,128)} %bitcast.70), calls=%async_computation.3 | async-start | bytes 16384 | tf_op jit(solution)/shard_map/all_to_all | solution.py:134
  83.2 4.5 reduce-window.14
  89.3 4.9 scatter_custom_fusion.1
  94.2 6.9 %all-to-all-start = ((s32[16,1,128]{2,1,0:T(1,128)}), s32[16,1,128]{2,1,0:T(1,128)S(1)}, u32[]{:S(2)}, u32[]{:S(2)}) async-start(s32[16,1,128]{2,1,0:T(1,128)} %bitcast.35), calls=%async_computation | async-start | bytes 16384 | tf_op jit(solution)/shard_map/all_to_all | solution.py:116
  101.2 5.1 gather_fusion.7
  106.3 2.1 all-to-all-done
  108.4 4.9 all-to-all-start.5
  113.3 3.9 copy.101
  119.3 3.6 convolution_convert_fusion
  122.9 1.4 fusion.13
  125.3 5.1 gather_fusion.5
  130.4 6.3 all-to-all-done.5
  136.7 5.8 all-to-all-start.4
  143.1 3.8 collective-permute-start
  159.7 9.2 %gather_fusion.3 = bf16[2048,512]{1,0:T(8,128)(2,1)} fusion(bf16[128,512]{1,0:T(8,128)(2,1)S(1)} %copy.93, s32[2048]{0:T(1024)S(1)} %fusion.24), kind=kCustom, calls=%fused_computation.3 | custom fusion | bytes 4202496 | tf_op jit(solution)/shard_map/gather | solution.py:119
  168.9 9.2 %gather_fusion.1 = bf16[2048,512]{1,0:T(8,128)(2,1)} fusion(bf16[128,512]{1,0:T(8,128)(2,1)S(1)} %copy.91, s32[2048]{0:T(1024)S(1)} %fusion.24), kind=kCustom, calls=%fused_computation.1 | custom fusion | bytes 4202496 | tf_op jit(solution)/shard_map/gather | solution.py:117
  179.3 7.7 %all-to-all-start.2 = ((bf16[16,128,512]{2,1,0:T(8,128)(2,1)}), bf16[16,128,512]{2,1,0:T(8,128)(2,1)}, u32[]{:S(2)}, u32[]{:S(2)}) async-start(bf16[16,128,512]{2,1,0:T(8,128)(2,1)} %bitcast.220), calls=%async_computation.2 | async-start | bytes 4194304 | tf_op jit(solution)/shard_map/all_to_all | solution.py:118
  187.0 318.6 %while.10 = (s32[]{:T(128)}, f32[16,8,8,256]{3,2,1,0:T(8,128)}, s32[16,8,6]{1,0,2:T(8,128)S(1)}, bf16[136,16,256]{2,1,0:T(8,128)(2,1)}, bf16[16,8,8,256]{3,2,1,0:T(8,128)(2,1)S(1)}, /*index=5*/s32[]{:T(128)}) while((s32[]{:T(128)}, f32[16,8,8,256]{3,2,1,0:T(8,128)}, s32[16,8,6]{1,0,2:T(8,128)S(1)}, bf16[136,16,256]{2,1,0:T(8,128)(2,1)}, ...), condition=%wide.region_9.10_spmd, body=%wide.region_8.9_spmd.sunk | while | flops 138527888 | bytes 4102221 | solution.py:110
  187.2 1.9 gather_fusion
  189.6 17.4 %fusion.54 = f32[16,8,8,256]{3,2,1,0:T(8,128)} fusion(f32[16,8,8,256]{3,2,1,0:T(8,128)} %get-tuple-element.202, s32[]{:T(128)} %get-tuple-element.201, f32[8,6,256]{2,1,0:T(8,128)S(1)} %get-tuple-element.173, f32[8,256]{1,0:T(8,128)S(1)} %get-tuple-element.174, f32[8,6,256]{2,1,0:T(8,128)S(1)} %get-tuple-element.175, ...), kind=kOutput, calls=%fused_computation.14.clone.1 | convolution fusion | flops 138412032 | bytes 852480 | tf_op jit(solution)/shard_map/while/body/eval_jaxpr/gjcs,gjts->gct/dot_general | solution.py:106
  207.2 1.8 gather_fusion
  209.5 17.4 %fusion.54 = f32[16,8,8,256]{3,2,1,0:T(8,128)} fusion(f32[16,8,8,256]{3,2,1,0:T(8,128)} %get-tuple-element.202, s32[]{:T(128)} %get-tuple-element.201, f32[8,6,256]{2,1,0:T(8,128)S(1)} %get-tuple-element.173, f32[8,256]{1,0:T(8,128)S(1)} %get-tuple-element.174, f32[8,6,256]{2,1,0:T(8,128)S(1)} %get-tuple-element.175, ...), kind=kOutput, calls=%fused_computation.14.clone.1 | convolution fusion | flops 138412032 | bytes 852480 | tf_op jit(solution)/shard_map/while/body/eval_jaxpr/gjcs,gjts->gct/dot_general | solution.py:106
  227.1 1.8 gather_fusion
  229.4 17.4 %fusion.54 = f32[16,8,8,256]{3,2,1,0:T(8,128)} fusion(f32[16,8,8,256]{3,2,1,0:T(8,128)} %get-tuple-element.202, s32[]{:T(128)} %get-tuple-element.201, f32[8,6,256]{2,1,0:T(8,128)S(1)} %get-tuple-element.173, f32[8,256]{1,0:T(8,128)S(1)} %get-tuple-element.174, f32[8,6,256]{2,1,0:T(8,128)S(1)} %get-tuple-element.175, ...), kind=kOutput, calls=%fused_computation.14.clone.1 | convolution fusion | flops 138412032 | bytes 852480 | tf_op jit(solution)/shard_map/while/body/eval_jaxpr/gjcs,gjts->gct/dot_general | solution.py:106
  247.0 1.8 gather_fusion
  249.3 17.4 %fusion.54 = f32[16,8,8,256]{3,2,1,0:T(8,128)} fusion(f32[16,8,8,256]{3,2,1,0:T(8,128)} %get-tuple-element.202, s32[]{:T(128)} %get-tuple-element.201, f32[8,6,256]{2,1,0:T(8,128)S(1)} %get-tuple-element.173, f32[8,256]{1,0:T(8,128)S(1)} %get-tuple-element.174, f32[8,6,256]{2,1,0:T(8,128)S(1)} %get-tuple-element.175, ...), kind=kOutput, calls=%fused_computation.14.clone.1 | convolution fusion | flops 138412032 | bytes 852480 | tf_op jit(solution)/shard_map/while/body/eval_jaxpr/gjcs,gjts->gct/dot_general | solution.py:106
  266.9 1.8 gather_fusion
  269.2 17.4 %fusion.54 = f32[16,8,8,256]{3,2,1,0:T(8,128)} fusion(f32[16,8,8,256]{3,2,1,0:T(8,128)} %get-tuple-element.202, s32[]{:T(128)} %get-tuple-element.201, f32[8,6,256]{2,1,0:T(8,128)S(1)} %get-tuple-element.173, f32[8,256]{1,0:T(8,128)S(1)} %get-tuple-element.174, f32[8,6,256]{2,1,0:T(8,128)S(1)} %get-tuple-element.175, ...), kind=kOutput, calls=%fused_computation.14.clone.1 | convolution fusion | flops 138412032 | bytes 852480 | tf_op jit(solution)/shard_map/while/body/eval_jaxpr/gjcs,gjts->gct/dot_general | solution.py:106
  286.8 1.8 gather_fusion
  289.1 17.4 %fusion.54 = f32[16,8,8,256]{3,2,1,0:T(8,128)} fusion(f32[16,8,8,256]{3,2,1,0:T(8,128)} %get-tuple-element.202, s32[]{:T(128)} %get-tuple-element.201, f32[8,6,256]{2,1,0:T(8,128)S(1)} %get-tuple-element.173, f32[8,256]{1,0:T(8,128)S(1)} %get-tuple-element.174, f32[8,6,256]{2,1,0:T(8,128)S(1)} %get-tuple-element.175, ...), kind=kOutput, calls=%fused_computation.14.clone.1 | convolution fusion | flops 138412032 | bytes 852480 | tf_op jit(solution)/shard_map/while/body/eval_jaxpr/gjcs,gjts->gct/dot_general | solution.py:106
  306.7 1.8 gather_fusion
  309.0 17.4 %fusion.54 = f32[16,8,8,256]{3,2,1,0:T(8,128)} fusion(f32[16,8,8,256]{3,2,1,0:T(8,128)} %get-tuple-element.202, s32[]{:T(128)} %get-tuple-element.201, f32[8,6,256]{2,1,0:T(8,128)S(1)} %get-tuple-element.173, f32[8,256]{1,0:T(8,128)S(1)} %get-tuple-element.174, f32[8,6,256]{2,1,0:T(8,128)S(1)} %get-tuple-element.175, ...), kind=kOutput, calls=%fused_computation.14.clone.1 | convolution fusion | flops 138412032 | bytes 852480 | tf_op jit(solution)/shard_map/while/body/eval_jaxpr/gjcs,gjts->gct/dot_general | solution.py:106
  326.6 1.8 gather_fusion
  328.9 17.4 %fusion.54 = f32[16,8,8,256]{3,2,1,0:T(8,128)} fusion(f32[16,8,8,256]{3,2,1,0:T(8,128)} %get-tuple-element.202, s32[]{:T(128)} %get-tuple-element.201, f32[8,6,256]{2,1,0:T(8,128)S(1)} %get-tuple-element.173, f32[8,256]{1,0:T(8,128)S(1)} %get-tuple-element.174, f32[8,6,256]{2,1,0:T(8,128)S(1)} %get-tuple-element.175, ...), kind=kOutput, calls=%fused_computation.14.clone.1 | convolution fusion | flops 138412032 | bytes 852480 | tf_op jit(solution)/shard_map/while/body/eval_jaxpr/gjcs,gjts->gct/dot_general | solution.py:106
  346.6 1.8 gather_fusion
  348.9 17.4 %fusion.54 = f32[16,8,8,256]{3,2,1,0:T(8,128)} fusion(f32[16,8,8,256]{3,2,1,0:T(8,128)} %get-tuple-element.202, s32[]{:T(128)} %get-tuple-element.201, f32[8,6,256]{2,1,0:T(8,128)S(1)} %get-tuple-element.173, f32[8,256]{1,0:T(8,128)S(1)} %get-tuple-element.174, f32[8,6,256]{2,1,0:T(8,128)S(1)} %get-tuple-element.175, ...), kind=kOutput, calls=%fused_computation.14.clone.1 | convolution fusion | flops 138412032 | bytes 852480 | tf_op jit(solution)/shard_map/while/body/eval_jaxpr/gjcs,gjts->gct/dot_general | solution.py:106
  366.5 1.8 gather_fusion
  368.8 17.4 %fusion.54 = f32[16,8,8,256]{3,2,1,0:T(8,128)} fusion(f32[16,8,8,256]{3,2,1,0:T(8,128)} %get-tuple-element.202, s32[]{:T(128)} %get-tuple-element.201, f32[8,6,256]{2,1,0:T(8,128)S(1)} %get-tuple-element.173, f32[8,256]{1,0:T(8,128)S(1)} %get-tuple-element.174, f32[8,6,256]{2,1,0:T(8,128)S(1)} %get-tuple-element.175, ...), kind=kOutput, calls=%fused_computation.14.clone.1 | convolution fusion | flops 138412032 | bytes 852480 | tf_op jit(solution)/shard_map/while/body/eval_jaxpr/gjcs,gjts->gct/dot_general | solution.py:106
  386.4 1.8 gather_fusion
  388.7 17.4 %fusion.54 = f32[16,8,8,256]{3,2,1,0:T(8,128)} fusion(f32[16,8,8,256]{3,2,1,0:T(8,128)} %get-tuple-element.202, s32[]{:T(128)} %get-tuple-element.201, f32[8,6,256]{2,1,0:T(8,128)S(1)} %get-tuple-element.173, f32[8,256]{1,0:T(8,128)S(1)} %get-tuple-element.174, f32[8,6,256]{2,1,0:T(8,128)S(1)} %get-tuple-element.175, ...), kind=kOutput, calls=%fused_computation.14.clone.1 | convolution fusion | flops 138412032 | bytes 852480 | tf_op jit(solution)/shard_map/while/body/eval_jaxpr/gjcs,gjts->gct/dot_general | solution.py:106
  406.3 1.8 gather_fusion
  408.6 17.4 %fusion.54 = f32[16,8,8,256]{3,2,1,0:T(8,128)} fusion(f32[16,8,8,256]{3,2,1,0:T(8,128)} %get-tuple-element.202, s32[]{:T(128)} %get-tuple-element.201, f32[8,6,256]{2,1,0:T(8,128)S(1)} %get-tuple-element.173, f32[8,256]{1,0:T(8,128)S(1)} %get-tuple-element.174, f32[8,6,256]{2,1,0:T(8,128)S(1)} %get-tuple-element.175, ...), kind=kOutput, calls=%fused_computation.14.clone.1 | convolution fusion | flops 138412032 | bytes 852480 | tf_op jit(solution)/shard_map/while/body/eval_jaxpr/gjcs,gjts->gct/dot_general | solution.py:106
  426.2 1.8 gather_fusion
  428.5 17.4 %fusion.54 = f32[16,8,8,256]{3,2,1,0:T(8,128)} fusion(f32[16,8,8,256]{3,2,1,0:T(8,128)} %get-tuple-element.202, s32[]{:T(128)} %get-tuple-element.201, f32[8,6,256]{2,1,0:T(8,128)S(1)} %get-tuple-element.173, f32[8,256]{1,0:T(8,128)S(1)} %get-tuple-element.174, f32[8,6,256]{2,1,0:T(8,128)S(1)} %get-tuple-element.175, ...), kind=kOutput, calls=%fused_computation.14.clone.1 | convolution fusion | flops 138412032 | bytes 852480 | tf_op jit(solution)/shard_map/while/body/eval_jaxpr/gjcs,gjts->gct/dot_general | solution.py:106
  446.1 1.8 gather_fusion
  448.4 17.4 %fusion.54 = f32[16,8,8,256]{3,2,1,0:T(8,128)} fusion(f32[16,8,8,256]{3,2,1,0:T(8,128)} %get-tuple-element.202, s32[]{:T(128)} %get-tuple-element.201, f32[8,6,256]{2,1,0:T(8,128)S(1)} %get-tuple-element.173, f32[8,256]{1,0:T(8,128)S(1)} %get-tuple-element.174, f32[8,6,256]{2,1,0:T(8,128)S(1)} %get-tuple-element.175, ...), kind=kOutput, calls=%fused_computation.14.clone.1 | convolution fusion | flops 138412032 | bytes 852480 | tf_op jit(solution)/shard_map/while/body/eval_jaxpr/gjcs,gjts->gct/dot_general | solution.py:106
  466.0 1.8 gather_fusion
  468.3 17.4 %fusion.54 = f32[16,8,8,256]{3,2,1,0:T(8,128)} fusion(f32[16,8,8,256]{3,2,1,0:T(8,128)} %get-tuple-element.202, s32[]{:T(128)} %get-tuple-element.201, f32[8,6,256]{2,1,0:T(8,128)S(1)} %get-tuple-element.173, f32[8,256]{1,0:T(8,128)S(1)} %get-tuple-element.174, f32[8,6,256]{2,1,0:T(8,128)S(1)} %get-tuple-element.175, ...), kind=kOutput, calls=%fused_computation.14.clone.1 | convolution fusion | flops 138412032 | bytes 852480 | tf_op jit(solution)/shard_map/while/body/eval_jaxpr/gjcs,gjts->gct/dot_general | solution.py:106
  485.9 1.8 gather_fusion
  488.2 17.4 %fusion.54 = f32[16,8,8,256]{3,2,1,0:T(8,128)} fusion(f32[16,8,8,256]{3,2,1,0:T(8,128)} %get-tuple-element.202, s32[]{:T(128)} %get-tuple-element.201, f32[8,6,256]{2,1,0:T(8,128)S(1)} %get-tuple-element.173, f32[8,256]{1,0:T(8,128)S(1)} %get-tuple-element.174, f32[8,6,256]{2,1,0:T(8,128)S(1)} %get-tuple-element.175, ...), kind=kOutput, calls=%fused_computation.14.clone.1 | convolution fusion | flops 138412032 | bytes 852480 | tf_op jit(solution)/shard_map/while/body/eval_jaxpr/gjcs,gjts->gct/dot_general | solution.py:106
  505.6 3.9 gather_fusion.8
  509.6 1.8 reshape.336
  511.4 3.9 gather_fusion.6
  515.9 10.4 %fusion.35 = (f32[64,8,1,64]{3,2,1,0:T(1,128)S(1)}, f32[64,8,1,64]{3,2,1,0:T(1,128)}, f32[64,8,1,64]{3,2,1,0:T(1,128)}, f32[64,8,1,64]{3,2,1,0:T(1,128)}, f32[64...) fusion(f32[64,8,8,64]{3,2,1,0:T(8,128)} %reshape.336), kind=kLoop, calls=%fused_computation.113 | loop fusion | bytes 2097152 | tf_op jit(solution)/shard_map/slice | solution.py:36
  526.3 6.9 %all-to-all-start.1 = ((bf16[16,128,512]{2,1,0:T(8,128)(2,1)}), bf16[16,128,512]{2,1,0:T(8,128)(2,1)S(1)}, u32[]{:S(2)}, u32[]{:S(2)}) async-start(bf16[16,128,512]{2,1,0:T(8,128)(2,1)} %bitcast.219), calls=%async_computation.1 | async-start | bytes 4194304 | tf_op jit(solution)/shard_map/all_to_all | solution.py:117
  533.2 25.4 %fusion.14 = bf16[64,8,64]{2,1,0:T(8,128)(2,1)} fusion(bf16[64,8,8,64]{3,2,1,0:T(8,128)(2,1)S(1)} %reshape.321, f32[64,8,64]{2,1,0:T(8,128)} %bitcast.237, f32[64,64]{1,0:T(8,128)S(1)} %bitcast.246, f32[64,8,64]{2,1,0:T(8,128)} %bitcast.238, f32[64,64]{1,0:T(8,128)S(1)} %bitcast.247, f32[64,8,64]{2,1,0:T(8,128)} %bitcast.239, f32[64,64]{1,0:T(8,128)S(1)} %bitcast.248, ...), kind=kOutput, calls=%fused_computation.53 | convolution fusion | flops 92307456 | bytes 1769472 | tf_op jit(solution)/shard_map/nfcb,nfab->nca/dot_general | solution.py:46
  558.7 13.8 %gather_fusion.4 = bf16[1024,512]{1,0:T(8,128)(2,1)S(1)} fusion(bf16[16,128,512]{2,1,0:T(8,128)(2,1)} %all-to-all-done.2, s32[1024]{0:T(1024)S(1)} %bitcast.211), kind=kCustom, calls=%fused_computation.4 | custom fusion | bytes 2105344 | tf_op jit(solution)/shard_map/gather | solution.py:122
  572.5 2.4 reshape.334
  574.9 17.5 %fusion.34 = (f32[128,8,1,64]{3,2,1,0:T(1,128)}, f32[128,8,1,64]{3,2,1,0:T(1,128)}, f32[128,8,1,64]{3,2,1,0:T(1,128)}, f32[128,8,1,64]{3,2,1,0:T(1,128)}, f32[12...) fusion(f32[128,8,8,64]{3,2,1,0:T(8,128)} %reshape.334), kind=kLoop, calls=%fused_computation.112 | loop fusion | bytes 4194304 | tf_op jit(solution)/shard_map/slice | solution.py:36
  592.4 7.3 %gather_fusion.2 = bf16[1024,512]{1,0:T(8,128)(2,1)S(1)} fusion(bf16[16,128,512]{2,1,0:T(8,128)(2,1)S(1)} %all-to-all-done.1, s32[1024]{0:T(1024)S(1)} %bitcast.212), kind=kCustom, calls=%fused_computation.2 | custom fusion | bytes 2105344 | tf_op jit(solution)/shard_map/gather | solution.py:121
  599.7 2.1 reshape.313
  601.8 45.6 %fusion.10 = f32[128,8,64]{2,1,0:T(8,128)} fusion(bf16[128,8,8,64]{3,2,1,0:T(8,128)(2,1)} %reshape.313, f32[128,8,64]{2,1,0:T(8,128)} %bitcast.227, f32[128,64]{1,0:T(8,128)S(1)} %copy-done.16, f32[128,8,64]{2,1,0:T(8,128)} %bitcast.228, f32[128,64]{1,0:T(8,128)} %copy.99, f32[128,8,64]{2,1,0:T(8,128)} %bitcast.229, f32[128,64]{1,0:T(8,128)} %copy.98, ...), kind=kOutput, calls=%fused_computation.47 | convolution fusion | flops 184549376 | bytes 3670016 | tf_op jit(solution)/shard_map/nfcb,nfab->nca/dot_general | solution.py:46
  647.5 5.1 fusion.9
  (337 shorter events, 34.2 us)
Async XLA Ops:
  0.0 88.7 %copy-start.29 = (s32[2]{0:T(128)S(1)}, s32[2]{0:T(128)}, u32[]{:S(2)}) copy-start(s32[2]{0:T(128)} %constant.21) | copy-start | bytes 28
  0.0 88.8 %copy-start.28 = (s32[2]{0:T(128)S(1)}, s32[2]{0:T(128)}, u32[]{:S(2)}) copy-start(s32[2]{0:T(128)} %constant.42) | copy-start | bytes 28
  0.0 82.8 %copy-start.24 = (s32[128,8]{0,1:T(8,128)S(1)}, s32[128,8]{0,1:T(8,128)}, u32[]{:S(2)}) copy-start(s32[128,8]{0,1:T(8,128)} %param.22) | copy-start | bytes 12292
  0.0 88.9 %copy-start.12 = (bf16[64,8,64]{2,1,0:T(8,128)(2,1)S(1)}, bf16[64,8,64]{2,1,0:T(8,128)(2,1)}, u32[]{:S(2)}) copy-start(bf16[64,8,64]{2,1,0:T(8,128)(2,1)} %param.20) | copy-start | bytes 196612
  0.0 89.1 %copy-start.25 = (s32[128,8]{0,1:T(8,128)S(1)}, s32[128,8]{0,1:T(8,128)}, u32[]{:S(2)}) copy-start(s32[128,8]{0,1:T(8,128)} %param.23) | copy-start | bytes 12292
  74.3 19.9 %all-to-all-start.3 = ((s32[16,1,64]{2,1,0:T(1,128)}), s32[16,1,64]{2,1,0:T(1,128)S(1)}, u32[]{:S(2)}, u32[]{:S(2)}) async-start(s32[16,1,64]{2,1,0:T(1,128)} %bitcast.70), calls=%async_computation.3 | async-start | bytes 16384 | tf_op jit(solution)/shard_map/all_to_all | solution.py:134
  94.2 14.2 %all-to-all-start = ((s32[16,1,128]{2,1,0:T(1,128)}), s32[16,1,128]{2,1,0:T(1,128)S(1)}, u32[]{:S(2)}, u32[]{:S(2)}) async-start(s32[16,1,128]{2,1,0:T(1,128)} %bitcast.35), calls=%async_computation | async-start | bytes 16384 | tf_op jit(solution)/shard_map/all_to_all | solution.py:116
  106.3 11.0 %copy-start.27 = (s32[128]{0:T(128)S(1)}, s32[128]{0:T(128)}, u32[]{:S(2)}) copy-start(s32[128]{0:T(128)} %param.16) | copy-start | bytes 1540
  108.4 28.3 %all-to-all-start.5 = ((bf16[16,64,512]{2,1,0:T(8,128)(2,1)}), bf16[16,64,512]{2,1,0:T(8,128)(2,1)S(1)}, u32[]{:S(2)}, u32[]{:S(2)}) async-start(bf16[16,64,512]{2,1,0:T(8,128)(2,1)} %bitcast.76), calls=%async_computation.5 | async-start | bytes 2097152 | tf_op jit(solution)/shard_map/all_to_all | solution.py:136
  117.3 7.0 %copy-start.6 = (bf16[128,64,64]{2,1,0:T(8,128)(2,1)}, bf16[128,64,64]{2,1,0:T(8,128)(2,1)S(1)}, u32[]{:S(2)}) copy-start(bf16[128,64,64]{2,1,0:T(8,128)(2,1)S(1)} %copy.101) | copy-start | bytes 3145732
  117.4 0.8 copy-start.13
  119.3 3.6 copy-start.8
  125.3 17.2 %copy-start.9 = (bf16[128,8,256]{2,1,0:T(8,128)(2,1)S(1)}, bf16[128,8,256]{2,1,0:T(8,128)(2,1)}, u32[]{:S(2)}) copy-start(bf16[128,8,256]{2,1,0:T(8,128)(2,1)} %copy-done.8) | copy-start | bytes 1572868
  125.3 17.2 %copy-start.10 = (bf16[128,8,256]{2,1,0:T(8,128)(2,1)S(1)}, bf16[128,8,256]{2,1,0:T(8,128)(2,1)}, u32[]{:S(2)}) copy-start(bf16[128,8,256]{2,1,0:T(8,128)(2,1)} %param.14) | copy-start | bytes 1572868
  130.4 27.5 %copy-start.26 = (s32[128,6]{0,1:T(8,128)S(1)}, s32[128,6]{0,1:T(8,128)}, u32[]{:S(2)}) copy-start(s32[128,6]{0,1:T(8,128)} %param.21) | copy-start | bytes 9220
  136.7 12.5 %copy-start.2 = (bf16[16,64,512]{2,1,0:T(8,128)(2,1)}, bf16[16,64,512]{2,1,0:T(8,128)(2,1)S(1)}, u32[]{:S(2)}) copy-start(bf16[16,64,512]{2,1,0:T(8,128)(2,1)S(1)} %all-to-all-done.5) | copy-start | bytes 3145732
  136.7 42.6 %all-to-all-start.4 = ((bf16[16,64,512]{2,1,0:T(8,128)(2,1)}), bf16[16,64,512]{2,1,0:T(8,128)(2,1)S(1)}, u32[]{:S(2)}, u32[]{:S(2)}) async-start(bf16[16,64,512]{2,1,0:T(8,128)(2,1)} %bitcast.221), calls=%async_computation.4 | async-start | bytes 2097152 | tf_op jit(solution)/shard_map/all_to_all | solution.py:135
  143.1 34.9 %collective-permute-start = (bf16[4,16,256]{2,1,0:T(8,128)(2,1)}, bf16[4,16,256]{2,1,0:T(8,128)(2,1)S(1)}, u32[]{:S(2)}, u32[]{:S(2)}) collective-permute-start(bf16[4,16,256]{2,1,0:T(8,128)(2,1)} %get-tuple-element.95), channel_id=1, source_target_pairs={{0,2},{2,4},{4,6},{6,8},{8,10},{10,12},{12,14},{14,16},{16,18},{18... | collective-permute-start | bytes 98312 | tf_op jit(solution)/shard_map/ppermute | solution.py:24
  147.0 31.1 %collective-permute-start.1 = (bf16[4,16,256]{2,1,0:T(8,128)(2,1)}, bf16[4,16,256]{2,1,0:T(8,128)(2,1)S(1)}, u32[]{:S(2)}, u32[]{:S(2)}) collective-permute-start(bf16[4,16,256]{2,1,0:T(8,128)(2,1)} %get-tuple-element.96), channel_id=1, source_target_pairs={{2,0},{4,2},{6,4},{8,6},{10,8},{12,10},{14,12},{16,14},{18,16},{20... | collective-permute-start | bytes 98312 | tf_op jit(solution)/shard_map/ppermute | solution.py:26
  179.3 7.7 %copy-start.4 = (bf16[16,64,512]{2,1,0:T(8,128)(2,1)}, bf16[16,64,512]{2,1,0:T(8,128)(2,1)S(1)}, u32[]{:S(2)}) copy-start(bf16[16,64,512]{2,1,0:T(8,128)(2,1)S(1)} %all-to-all-done.4) | copy-start | bytes 3145732
  179.3 347.1 %all-to-all-start.2 = ((bf16[16,128,512]{2,1,0:T(8,128)(2,1)}), bf16[16,128,512]{2,1,0:T(8,128)(2,1)}, u32[]{:S(2)}, u32[]{:S(2)}) async-start(bf16[16,128,512]{2,1,0:T(8,128)(2,1)} %bitcast.220), calls=%async_computation.2 | async-start | bytes 4194304 | tf_op jit(solution)/shard_map/all_to_all | solution.py:118
  187.0 318.7 %copy-start.1 = (s32[512,1]{0,1:T(1,128)S(1)}, s32[512,1]{0,1:T(1,128)}, u32[]{:S(2)}) copy-start(s32[512,1]{0,1:T(1,128)} %get-tuple-element.54) | copy-start | bytes 6148
  187.0 318.7 %copy-start.3 = (bf16[16,64,512]{2,1,0:T(8,128)(2,1)S(1)}, bf16[16,64,512]{2,1,0:T(8,128)(2,1)}, u32[]{:S(2)}) copy-start(bf16[16,64,512]{2,1,0:T(8,128)(2,1)} %copy-done.2) | copy-start | bytes 3145732
  505.6 5.8 copy-start.5
  515.9 17.3 %copy-start.20 = (f32[64,1,1,64]{3,2,0,1:T(1,128)S(1)}, f32[64,1,1,64]{3,2,0,1:T(1,128)}, u32[]{:S(2)}) copy-start(f32[64,1,1,64]{3,2,0,1:T(1,128)} %get-tuple-element.97) | copy-start | bytes 49156
  515.9 17.3 %copy-start.21 = (f32[64,1,1,64]{3,2,0,1:T(1,128)S(1)}, f32[64,1,1,64]{3,2,0,1:T(1,128)}, u32[]{:S(2)}) copy-start(f32[64,1,1,64]{3,2,0,1:T(1,128)} %get-tuple-element.98) | copy-start | bytes 49156
  515.9 17.3 %copy-start.22 = (f32[64,1,1,64]{3,2,0,1:T(1,128)S(1)}, f32[64,1,1,64]{3,2,0,1:T(1,128)}, u32[]{:S(2)}) copy-start(f32[64,1,1,64]{3,2,0,1:T(1,128)} %get-tuple-element.99) | copy-start | bytes 49156
  515.9 17.3 %copy-start.23 = (f32[64,1,1,64]{3,2,0,1:T(1,128)S(1)}, f32[64,1,1,64]{3,2,0,1:T(1,128)}, u32[]{:S(2)}) copy-start(f32[64,1,1,64]{3,2,0,1:T(1,128)} %get-tuple-element.100) | copy-start | bytes 49156
  526.3 66.1 %all-to-all-start.1 = ((bf16[16,128,512]{2,1,0:T(8,128)(2,1)}), bf16[16,128,512]{2,1,0:T(8,128)(2,1)S(1)}, u32[]{:S(2)}, u32[]{:S(2)}) async-start(bf16[16,128,512]{2,1,0:T(8,128)(2,1)} %bitcast.219), calls=%async_computation.1 | async-start | bytes 4194304 | tf_op jit(solution)/shard_map/all_to_all | solution.py:117
  533.2 25.4 %copy-start = (s32[1024,1]{0,1:T(1,128)S(1)}, s32[1024,1]{0,1:T(1,128)}, u32[]{:S(2)}) copy-start(s32[1024,1]{0,1:T(1,128)} %get-tuple-element.113) | copy-start | bytes 12292
  592.3 9.4 %copy-start.16 = (f32[128,64]{1,0:T(8,128)S(1)}, f32[128,64]{1,0:T(8,128)}, u32[]{:S(2)}) copy-start(f32[128,64]{1,0:T(8,128)} %copy.100) | copy-start | bytes 98308
  592.4 9.4 %copy-start.17 = (f32[128,64]{1,0:T(8,128)S(1)}, f32[128,64]{1,0:T(8,128)}, u32[]{:S(2)}) copy-start(f32[128,64]{1,0:T(8,128)} %copy.92) | copy-start | bytes 98308
  592.4 9.4 %copy-start.18 = (f32[128,64]{1,0:T(8,128)S(1)}, f32[128,64]{1,0:T(8,128)}, u32[]{:S(2)}) copy-start(f32[128,64]{1,0:T(8,128)} %copy.94) | copy-start | bytes 98308
  592.4 9.4 %copy-start.19 = (f32[128,64]{1,0:T(8,128)S(1)}, f32[128,64]{1,0:T(8,128)}, u32[]{:S(2)}) copy-start(f32[128,64]{1,0:T(8,128)} %copy.95) | copy-start | bytes 98308
  601.8 45.6 %copy-start.15 = (bf16[64,8,64]{2,1,0:T(8,128)(2,1)S(1)}, bf16[64,8,64]{2,1,0:T(8,128)(2,1)}, u32[]{:S(2)}) copy-start(bf16[64,8,64]{2,1,0:T(8,128)(2,1)} %fusion.14) | copy-start | bytes 196612
  601.8 45.7 %copy-start.7 = (bf16[128,64,64]{2,1,0:T(8,128)(2,1)S(1)}, bf16[128,64,64]{2,1,0:T(8,128)(2,1)}, u32[]{:S(2)}) copy-start(bf16[128,64,64]{2,1,0:T(8,128)(2,1)} %copy-done.6) | copy-start | bytes 3145732
  601.8 45.7 %copy-start.11 = (f32[16,8,8,256]{3,2,1,0:T(8,128)S(1)}, f32[16,8,8,256]{3,2,1,0:T(8,128)}, u32[]{:S(2)}) copy-start(f32[16,8,8,256]{3,2,1,0:T(8,128)} %get-tuple-element.32) | copy-start | bytes 3145732
  601.8 45.6 %copy-start.14 = (pred[128,256]{1,0:T(8,128)(4,1)S(1)}, pred[128,256]{1,0:T(8,128)(4,1)}, u32[]{:S(2)}) copy-start(pred[128,256]{1,0:T(8,128)(4,1)} %copy-done.13) | copy-start | bytes 98308
where the time goes:
time: 656 us; the launch traced here: 653 us
  matrix products  360 us (55%)
  local copies, waits for them, and re-layouts  224 us (34%)
  starting transfers between devices  45.8 us (7%)
  other arithmetic  13.2 us (2%)
  waiting for transfers between devices  8.37 us (1%)
    dot_general x16, matrix products, near_block(): jnp.einsum('gjcs,gjts->gct', source_rows[:, :, DIM:], kernel, preferred_e...  279 us
    dot_general x2, matrix products, far_sum(): jnp.einsum('nfcb,nfab->nca', source_coef, kernel, preferred_element_type=...  71 us
    scatter x1, local copies, waits for them, and re-layouts, slot_table(): jnp.zeros((owners, capacity), jnp.int32).at[flat_owner, slot_index]  69.6 us
    slice x19, local copies, waits for them, and re-layouts, matern(): offset = targets[..., coord, :, None] - sources[..., coord, None, :]  33 us
    gather x16, local copies, waits for them, and re-layouts, near_block(): source_rows = extended[chosen]  29.3 us
    gather x1, local copies, waits for them, and re-layouts, body(): picked_skel = got_skel[flat_owner, slot_index]  13.8 us
  transfers between devices with their start and end apart: 8, of which 2 were waited for; matrix products, arithmetic and copies ran while one was open for 71% of the time, Pallas kernels for 0%

commit v1 on v0

v1 whole, which is shorter than its diff:
```python
import math

import jax
import jax.numpy as jnp
from jax import lax
from jax.experimental import pallas as pl
from jax.experimental.pallas import tpu as pltpu
from jax.sharding import PartitionSpec as P

HALO = 4
UNROLL = 16
S_SCALE = math.sqrt(3.0) / 1.5
EXP_SCALE = -S_SCALE / math.log(2.0)
TINY = 1e-12
VMEM = 56 * 1024 * 1024


def norm_rows(coords):
    row = lax.broadcasted_iota(jnp.int32, coords.shape, 0)
    norm = jnp.sum(coords * coords, axis=0, keepdims=True)
    high = norm.astype(jnp.bfloat16).astype(jnp.float32)
    rest = norm - high
    mid = rest.astype(jnp.bfloat16).astype(jnp.float32)
    ones = jnp.where((row >= 4) & (row < 7), 1.0, 0.0)
    return jnp.where(row == 0, high, jnp.where(row == 1, mid, jnp.where(row == 2, rest - mid, ones)))


def source_features(coords):
    return jnp.concatenate([coords, norm_rows(coords)], axis=0)


def target_features(coords):
    return jnp.concatenate([coords * -2.0, pltpu.roll(norm_rows(coords), 4, 0)], axis=0)


def matern(square):
    bounded = jnp.maximum(square, TINY)
    dist = bounded * lax.rsqrt(bounded)
    return ((1.0 + dist * S_SCALE) * jnp.exp2(dist * EXP_SCALE)).astype(jnp.bfloat16)


def prepare(count_ref, point_ref, value_ref, basis_ref, transfer_ref, feat_ref, masked_ref, coef_ref, upper_ref):
    leaves, columns, leaf_size = value_ref.shape
    base = pl.program_id(0) * leaves
    lane = lax.broadcasted_iota(jnp.int32, (columns, leaf_size), 1)
    parent = None
    for u in range(leaves):
        feat_ref[u] = source_features(point_ref[u].astype(jnp.float32)).astype(jnp.bfloat16)
        kept = jnp.where(lane < count_ref[base + u], value_ref[u].astype(jnp.float32), 0.0)
        kept = kept.astype(jnp.bfloat16)
        masked_ref[u] = kept
        coef = lax.dot_general(
            kept, basis_ref[u], (((1,), (1,)), ((), ())), preferred_element_type=jnp.float32
        ).astype(jnp.bfloat16)
        coef_ref[u] = coef
        term = jnp.dot(coef, transfer_ref[u], preferred_element_type=jnp.float32)
        if u % 2 == 0:
            parent = term
        else:
            upper_ref[u // 2] = (parent + term).astype(jnp.bfloat16)


def near_kernel(near, offset, ids_ref, feat_ref, val_ref, _, out_ref, done_ref):
    done_ref[0] = 0
    leaves = out_ref.shape[0]
    pair = math.gcd(leaves, 2)

    def group(g, _):
        for u in range(pair):
            l = g * pair + u
            base = (offset + l) * near
            own = feat_ref[ids_ref[base]].astype(jnp.float32)
            target = jnp.concatenate([own[0:8] * -2.0, pltpu.roll(own[8:16], 4, 0)], axis=0)
            target = target.astype(jnp.bfloat16)
            total = None
            for j in range(near):
                q = ids_ref[base + j]
                square = lax.dot_general(
                    feat_ref[q],
                    target,
                    (((0,), (0,)), ((), ())),
                    preferred_element_type=jnp.float32,
                )
                part = jnp.dot(val_ref[q], matern(square), preferred_element_type=jnp.float32)
                total = part if total is None else total + part
            out_ref[l] = total
        return 0

    lax.fori_loop(0, leaves // pair, group, 0)


def pick_pair(row_ref, half_ref, rows_ref, first, lane):
    rank = rows_ref.shape[2] // 2
    left = rows_ref[row_ref[first]].astype(jnp.float32)
    right = rows_ref[row_ref[first + 1]].astype(jnp.float32)
    left = pltpu.roll(left, half_ref[first] * rank, 1)
    right = pltpu.roll(right, (1 - half_ref[first + 1]) * rank, 1)
    return jnp.where(lane < rank, left, right)


def far_kernel_matrix(far, row_ref, half_ref, target_ref, rows_ref, out_ref):
    lane = lax.broadcasted_iota(jnp.int32, rows_ref.shape[1:], 1)
    unroll = out_ref.shape[0]
    for u in range(unroll):
        base = (pl.program_id(0) * unroll + u) * far
        sources = [
            source_features(pick_pair(row_ref, half_ref, rows_ref, base + f, lane)).astype(jnp.bfloat16)
            for f in range(0, far, 2)
        ]
        target = target_features(target_ref[u].astype(jnp.float32)).T.astype(jnp.bfloat16)
        square = jnp.dot(
            target, jnp.concatenate(sources, axis=1), preferred_element_type=jnp.float32
        )
        out_ref[u] = matern(square)


def far_apply(far, row_ref, half_ref, matrix_ref, rows_ref, out_ref):
    lane = lax.broadcasted_iota(jnp.int32, rows_ref.shape[1:], 1)
    unroll = out_ref.shape[0]
    for u in range(unroll):
        base = (pl.program_id(0) * unroll + u) * far
        coefs = [
            pick_pair(row_ref, half_ref, rows_ref, base + f, lane).astype(jnp.bfloat16)
            for f in range(0, far, 2)
        ]
        out_ref[u] = lax.dot_general(
            jnp.concatenate(coefs, axis=1),
            matrix_ref[u],
            (((1,), (1,)), ((), ())),
            preferred_element_type=jnp.float32,
        )


def paired(bundle):
    half = bundle.shape[0] // 2
    return jnp.concatenate([bundle[:half], bundle[half:]], axis=2)


def body(
    points,
    values,
    counts,
    leaf_basis,
    transfer,
    leaf_skeleton,
    upper_skeleton,
    near_list,
    far_owner,
    far_local,
    upper_owner,
    upper_local,
):
    leaf_dev, _, leaf_size = points.shape
    columns = values.shape[1]
    rank = leaf_basis.shape[1]
    far = far_owner.shape[1]
    near = near_list.shape[1]
    par_dev = leaf_dev // 2
    half = leaf_dev // 2
    upper_half = par_dev // 2
    block = half + upper_half
    count = lax.axis_size("leaf")
    side = lax.axis_index("rhs")
    swap = [(0, 1), (1, 0)]

    smem = pl.BlockSpec(memory_space=pltpu.SMEM)
    vmem = pl.BlockSpec(memory_space=pltpu.VMEM)
    params = pltpu.CompilerParams(vmem_limit_bytes=VMEM)

    group = math.gcd(leaf_dev, UNROLL)
    feats, masked, leaf_coef, upper_coef = pl.pallas_call(
        prepare,
        grid=(leaf_dev // group,),
        in_specs=[
            smem,
            pl.BlockSpec((group, 8, leaf_size), lambda g: (g, 0, 0)),
            pl.BlockSpec((group, columns, leaf_size), lambda g: (g, 0, 0)),
            pl.BlockSpec((group, rank, leaf_size), lambda g: (g, 0, 0)),
            pl.BlockSpec((group, rank, rank), lambda g: (g, 0, 0)),
        ],
        out_specs=[
            pl.BlockSpec((group, 16, leaf_size), lambda g: (g, 0, 0)),
            pl.BlockSpec((group, columns, leaf_size), lambda g: (g, 0, 0)),
            pl.BlockSpec((group, columns, rank), lambda g: (g, 0, 0)),
            pl.BlockSpec((group // 2, columns, rank), lambda g: (g, 0, 0)),
        ],
        out_shape=[
            jax.ShapeDtypeStruct((leaf_dev, 16, leaf_size), jnp.bfloat16),
            jax.ShapeDtypeStruct((leaf_dev, columns, leaf_size), jnp.bfloat16),
            jax.ShapeDtypeStruct((leaf_dev, columns, rank), jnp.bfloat16),
            jax.ShapeDtypeStruct((par_dev, columns, rank), jnp.bfloat16),
        ],
        compiler_params=params,
        name="prepare",
    )(counts, points, values, leaf_basis, transfer)

    skeletons = jnp.concatenate([paired(leaf_skeleton), paired(upper_skeleton)], axis=0)
    piece = block // 2
    packed = jnp.concatenate(
        [
            paired(leaf_coef),
            paired(upper_coef),
            lax.dynamic_slice_in_dim(skeletons, side * piece, piece),
        ],
        axis=0,
    )[None]
    me = lax.axis_index("leaf")

    def across(cells, bits):
        return lax.ppermute(cells, "leaf", [(i, i ^ bits) for i in range(count)])

    def shifted(cells, step, other):
        pairs = [
            ((i * 2 + s), (i + step) * 2 + (s ^ other))
            for i in range(count)
            for s in range(2)
            if 0 <= i + step < count
        ]
        return lax.ppermute(cells, ("leaf", "rhs"), pairs)

    tail, head = slice(leaf_dev - HALO, leaf_dev), slice(0, HALO)
    before = shifted(jnp.concatenate([feats[tail], masked[tail]], axis=1), 1, 0)
    after = shifted(jnp.concatenate([feats[head], masked[head]], axis=1), -1, 0)
    partner = jnp.concatenate(
        [shifted(masked[tail], 1, 1), lax.ppermute(masked, "rhs", swap), shifted(masked[head], -1, 1)],
        axis=0,
    )
    feats = jnp.concatenate([before[:, :16], feats, after[:, :16]], axis=0)
    own_vals = jnp.concatenate([before[:, 16:], masked, after[:, 16:]], axis=0)
    vals = jnp.concatenate([own_vals, partner], axis=1)

    first_leaf = me * leaf_dev - HALO
    start = side * half
    near_ids = (lax.dynamic_slice_in_dim(near_list, start, half) - first_leaf).reshape(-1)

    def after_piece(done, cells):
        return jnp.where(done[0] == 0, cells, jnp.zeros_like(cells))

    def near_piece(offset, leaves, follows):
        work = leaves * near * leaf_size * leaf_size
        return pl.pallas_call(
            lambda *refs: near_kernel(near, offset, *refs),
            out_shape=[
                jax.ShapeDtypeStruct((leaves, 2 * columns, leaf_size), jnp.float32),
                jax.ShapeDtypeStruct((1,), jnp.int32),
            ],
            in_specs=[smem, vmem, vmem, pl.BlockSpec(memory_space=pl.ANY)],
            out_specs=[vmem, smem],
            compiler_params=params,
            cost_estimate=pl.CostEstimate(
                flops=work * 64, bytes_accessed=1 << 22, transcendentals=work * 2
            ),
            name="near_field",
        )(near_ids, feats, vals, follows)

    cuts = [0, half // 4, half * 5 // 8, half * 7 // 8, half]
    sizes = [cuts[i + 1] - cuts[i] for i in range(4)]
    if count == 16:
        apart = [across(packed, bits) for bits in (4, 8, 12)]
        near0, done = near_piece(cuts[0], sizes[0], packed)
        column = after_piece(done, jnp.concatenate([packed] + apart, axis=0))
        along_x, along_y = across(column, 1), across(column, 2)
        near1, done = near_piece(cuts[1], sizes[1], column)
        from_x, from_y = after_piece(done, along_x[:2]), after_piece(done, along_y[2:])
        diagonal = [across(from_x, 2), across(from_y, 1)]
        near2, done = near_piece(cuts[2], sizes[2], from_y)
        everything = jnp.concatenate([column, along_x, along_y] + diagonal, axis=0)

        def position(owner):
            apart_bits = owner ^ me
            return (apart_bits & 3) * 4 + (apart_bits >> 2)

    else:
        near0, near1, near2 = [near_piece(cuts[i], sizes[i], packed)[0] for i in range(3)]
        done = jnp.zeros((1,), jnp.int32)
        everything = lax.all_gather(packed, "leaf", axis=0, tiled=True)

        def position(owner):
            return owner
    coefs = everything[:, :block].reshape(count * block, columns, 2 * rank)
    half_skel = after_piece(done, everything[:, block:]).reshape(count * piece, 8, 2 * rank)
    skeletons = jnp.concatenate([half_skel, lax.ppermute(half_skel, "rhs", swap)], axis=0)
    near3, _ = near_piece(cuts[3], sizes[3], half_skel)
    near_half = jnp.concatenate([near0, near1, near2, near3], axis=0)
    mine = near_half[:, :columns]
    other = lax.ppermute(near_half[:, columns:], "rhs", swap)
    near_part = jnp.where(
        side == 0,
        jnp.concatenate([mine, other], axis=0),
        jnp.concatenate([other, mine], axis=0),
    )
    live = lax.broadcasted_iota(jnp.int32, (leaf_dev, leaf_size), 1) < counts[:, None]

    targets = jnp.concatenate([leaf_skeleton, upper_skeleton], axis=0)
    row_in_block = jnp.concatenate(
        [far_local % half, half + upper_local % upper_half], axis=0
    ).reshape(-1)
    place = position(jnp.concatenate([far_owner, upper_owner], axis=0).reshape(-1))
    row_ids = place * block + row_in_block
    skel_ids = (
        jnp.where(row_in_block // piece == side, 0, count * piece)
        + place * piece
        + row_in_block % piece
    )
    half_ids = jnp.concatenate([far_local // half, upper_local // upper_half], axis=0).reshape(-1)
    clusters = leaf_dev + par_dev
    unroll = math.gcd(clusters, UNROLL)
    pairs_far = clusters * far * rank * rank
    matrix_spec = pl.BlockSpec((unroll, rank, far * rank), lambda g: (g, 0, 0))
    matrix = pl.pallas_call(
        lambda *refs: far_kernel_matrix(far, *refs),
        grid=(clusters // unroll,),
        out_shape=jax.ShapeDtypeStruct((clusters, rank, far * rank), jnp.bfloat16),
        in_specs=[smem, smem, pl.BlockSpec((unroll, 8, rank), lambda g: (g, 0, 0)), vmem],
        out_specs=matrix_spec,
        compiler_params=params,
        cost_estimate=pl.CostEstimate(
            flops=pairs_far * 64, bytes_accessed=1 << 24, transcendentals=pairs_far * 2
        ),
        name="far_matrices",
    )(skel_ids, half_ids, targets, skeletons)
    field = pl.pallas_call(
        lambda *refs: far_apply(far, *refs),
        grid=(clusters // unroll,),
        out_shape=jax.ShapeDtypeStruct((clusters, columns, rank), jnp.float32),
        in_specs=[smem, smem, matrix_spec, vmem],
        out_specs=pl.BlockSpec((unroll, columns, rank), lambda g: (g, 0, 0)),
        compiler_params=params,
        cost_estimate=pl.CostEstimate(
            flops=pairs_far * 16, bytes_accessed=1 << 24, transcendentals=0
        ),
        name="far_apply",
    )(row_ids, half_ids, matrix, coefs)

    spread = jnp.repeat(field[leaf_dev:].astype(jnp.bfloat16), 2, axis=0)
    leaf_field = (
        field[:leaf_dev]
        + jnp.einsum("lcm,lkm->lck", spread, transfer, preferred_element_type=jnp.float32)
    ).astype(jnp.bfloat16)
    far_part = jnp.einsum(
        "lck,lkp->lcp", leaf_field, leaf_basis, preferred_element_type=jnp.float32
    )
    return jnp.where(live[:, None, :], far_part + near_part, 0.0)


def solution(mesh):
    return jax.shard_map(
        body,
        mesh=mesh,
        in_specs=(
            P("leaf", None, None),
            P("leaf", "rhs", None),
            P("leaf"),
            P("leaf", None, None),
            P("leaf", None, None),
            P("leaf", None, None),
            P("leaf", None, None),
            P("leaf", None),
            P("leaf", None),
            P("leaf", None),
            P("leaf", None),
            P("leaf", None),
        ),
        out_specs=P("leaf", "rhs", None),
        check_vma=False,
    )
```

time: 656 us -> 185 us (0.28)
  matrix products: 360 us -> 5.07 us
  local copies, waits for them, and re-layouts: 224 us -> 25.9 us
  Pallas kernels: 0 us -> 104 us
  starting transfers between devices: 45.8 us -> 25.6 us
    dot_general x20 -> x0, matrix products: 355 us -> none  [the longest x16 279 us: near_block(): jnp.einsum('gjcs,gjts->gct', source_rows[:, :, DIM:], kernel, preferred_e...]
    pallas_call x0 -> x7, Pallas kernels: none -> 104 us  [the longest x4 62 us: near_piece(): pl.pallas_call(lambda *refs: near_kernel(near, offset, *refs), out_shape=...]
    gather x24 -> x0, local copies, waits for them, and re-layouts: 86.7 us -> none  [the longest x16 29.3 us: near_block(): source_rows = extended[chosen]]
    scatter x1 -> x0, local copies, waits for them, and re-layouts: 69.6 us -> none  [slot_table(): jnp.zeros((owners, capacity), jnp.int32).at[flat_owner, slot_index]]
    all_to_all x6 -> x0, starting transfers between devices: 40.7 us -> none  [the longest x1 8.43 us: body(): lax.all_to_all(upper_wanted, 'leaf', split_axis=0, concat_axis=0, tiled=T...]
    slice x21 -> x13, local copies, waits for them, and re-layouts: 33.2 us -> 12.2 us  [the longest x1 3.94 us: body(): coefs = everything[:, :block].reshape(count * block, columns, 2 * rank)]
    ppermute x2 -> x14, starting transfers between devices: 5.11 us -> 25.6 us  [the longest x4 12.6 us: shifted(): return lax.ppermute(cells, ('leaf', 'rhs'), pairs)]
    concatenate x3 -> x7, other arithmetic: 2.37 us -> 11.5 us  [the longest x1 7.3 us: body(): jnp.concatenate([half_skel, lax.ppermute(half_skel, 'rhs', swap)], axis=0)]
  transfers between devices with their start and end apart: 8 -> 14, of which waited for: 2 -> 2; matrix products, arithmetic and copies ran while one was open for 71% -> 17% of each run, Pallas kernels for 0% -> 50%
where the time goes in v1:
time: 185 us; the launch traced here: 184 us
  Pallas kernels  104 us (56%)
  local copies, waits for them, and re-layouts  25.9 us (14%)
  starting transfers between devices  25.6 us (14%)
  other arithmetic  17.5 us (9%)
  matrix products  5.07 us (3%)
  waiting for transfers between devices  3.98 us (2%)
  between operations  2.42 us (1%)
    pallas_call x4, Pallas kernels, near_piece(): pl.pallas_call(lambda *refs: near_kernel(near, offset, *refs), out_shape=...  62 us
    pallas_call x1, Pallas kernels, body(): pl.pallas_call(lambda *refs: far_kernel_matrix(far, *refs), grid=(cluster...  16.7 us
    pallas_call x1, Pallas kernels, body(): pl.pallas_call(lambda *refs: far_apply(far, *refs), grid=(clusters // unr...  13 us
    ppermute x4, starting transfers between devices, shifted(): return lax.ppermute(cells, ('leaf', 'rhs'), pairs)  12.6 us
    pallas_call x1, Pallas kernels, body(): pl.pallas_call(prepare, grid=(leaf_dev // group,), in_specs=[smem, pl.Blo...  12 us
    ppermute x7, starting transfers between devices, across(): return lax.ppermute(cells, 'leaf', [(i, i ^ bits) for i in range(count)])  12 us
    unnamed x44, local copies, waits for them, and re-layouts  8.22 us
    concatenate x1, other arithmetic, body(): jnp.concatenate([half_skel, lax.ppermute(half_skel, 'rhs', swap)], axis=0)  7.3 us
  transfers between devices with their start and end apart: 14, of which 2 were waited for; matrix products, arithmetic and copies ran while one was open for 17% of the time, Pallas kernels for 50%

profile of v1, /device:TPU:0, one launch (start us, length us, event | category | flops | bytes accessed | tf_op | source)
XLA Modules:
  0.0 184.0 jit_solution(12039613445321162402)
XLA Ops:
  0.0 4.7 %copy.25.transfer_ref = bf16[128,64,64]{2,1,0:T(8,128)(2,1)} copy(bf16[128,64,64]{0,2,1:T(8,128)(2,1)} %param.16) | data formatting | bytes 2097152 | tf_op args[4]
  4.7 12.0 %prepare.1 = (bf16[128,16,256]{2,1,0:T(8,128)(2,1)}, bf16[128,8,256]{2,1,0:T(8,128)(2,1)}, bf16[128,8,64]{2,1,0:T(8,128)(2,1)}, bf16[64,8,64]{2,1,0:T(8,128)(2,1)}) custom-call(s32[128]{0:T(128)} %count_ref.1, bf16[128,8,256]{2,1,0:T(8,128)(2,1)} %point_ref.1, bf16[128,8,256]{2,1,0:T(8,128)(2,1)} %value_ref.1, bf16[128,64,256]{2,1,0:T(8,128)(2,1)} %basis_ref.1, ...), custom_call_target="tpu_custom_call" | custom-call | tf_op jit(solution)/shard_map/prepare/pallas_call | solution.py:171
  16.7 0.5 collective-permute-start.3
  17.2 0.7 fusion.20
  17.9 4.5 %collective-permute-start.2 = (bf16[4,8,256]{2,1,0:T(8,128)(2,1)S(1)}, bf16[4,8,256]{2,1,0:T(8,128)(2,1)S(1)}, u32[]{:S(2)}, u32[]{:S(2)}) collective-permute-start(bf16[4,8,256]{2,1,0:T(8,128)(2,1)S(1)} %get-tuple-element.33), channel_id=1, source_target_pairs={{0,3},{1,2},{2,5},{3,4},{4,7},{5,6},{6,9},{7,8},{8,11},{9,10},{10,... | collective-permute-start | bytes 49160 | tf_op jit(solution)/shard_map/ppermute | solution.py:219
  22.4 1.3 collective-permute-start.4
  23.7 0.8 fusion.19
  24.5 1.3 collective-permute-start.1
  25.8 5.5 %collective-permute-start = (bf16[4,24,256]{2,1,0:T(8,128)(2,1)S(1)}, bf16[4,24,256]{2,1,0:T(8,128)(2,1)}, u32[]{:S(2)}, u32[]{:S(2)}) collective-permute-start(bf16[4,24,256]{2,1,0:T(8,128)(2,1)S(1)} %pad_maximum_fusion.3), channel_id=1, source_target_pairs={{0,2},{1,3},{2,4},{3,5},{4,6},{5,7},{6,8},{7,9},{8,10},{9,11},{10,... | collective-permute-start | bytes 147464 | tf_op jit(solution)/shard_map/ppermute | solution.py:219
  31.3 0.2 copy.23
  31.6 1.0 fusion.21
  32.6 0.9 fusion.23
  33.5 0.4 fusion.8
  33.9 0.1 maximum_bitcast_fusion.refs_3_
  34.1 0.8 dynamic-slice_subtract_fusion
  35.0 0.7 reshape.51.refs_0_
  35.7 5.3 %collective-permute-start.7 = (bf16[1,144,8,128]{3,2,1,0:T(8,128)(2,1)S(1)}, bf16[1,144,8,128]{3,2,1,0:T(8,128)(2,1)S(1)}, u32[]{:S(2)}, u32[]{:S(2)}) collective-permute-start(bf16[1,144,8,128]{3,2,1,0:T(8,128)(2,1)S(1)} %maximum_bitcast_fusion.refs_3_), channel_id=1, source_target_pairs={{0,24},{2,26},{4,28},{6,30},{8,16},{10,18},{12,20},{14,22},{16,8},... | collective-permute-start | bytes 884744 | tf_op jit(solution)/shard_map/ppermute | solution.py:210
  41.1 0.8 slice.100
  41.8 0.8 slice.99
  42.6 0.6 collective-permute-start.5
  43.2 1.2 pad_maximum_fusion.1.refs_1_
  44.3 0.7 slice.102
  45.0 0.7 slice.101
  45.8 1.8 maximum_maximum_fusion.refs_2_
  47.6 15.6 %near_field.4 = (f32[16,16,256]{2,1,0:T(8,128)}, s32[1]{0:T(128)}) custom-call(s32[384]{0:T(512)} %reshape.51.refs_0_, bf16[136,16,256]{2,1,0:T(8,128)(2,1)} %pad_maximum_fusion.1.refs_1_, bf16[136,16,256]{2,1,0:T(8,128)(2,1)} %maximum_maximum_fusion.refs_2_, bf16[1,144,8,128]{3,2,1,0:T(8,128)(2,1)} %copy-done.5), custom_call_target="tpu_custom_call" | custom-call | flops 402653184 | bytes 4194304 | tf_op jit(solution)/shard_map/near_field/pallas_call | solution.py:241
  63.9 2.4 %collective-permute-done.6 = bf16[1,144,8,128]{3,2,1,0:T(8,128)(2,1)} collective-permute-done((bf16[1,144,8,128]{3,2,1,0:T(8,128)(2,1)S(1)}, bf16[1,144,8,128]{3,2,1,0:T(8,128)(2,1)}, u32[]{:S(2)}, u32[]{:S(2)}) %collective-permute-start.6) | collective-permute-done | bytes 294944 | tf_op jit(solution)/shard_map/ppermute | solution.py:210
  66.3 0.7 copy-done.9
  67.0 2.5 %constant_dynamic-update-slice_fusion.4 = (bf16[16,144,8,128]{3,2,1,0:T(8,128)(2,1)S(1)}, bf16[4,144,8,128]{3,2,1,0:T(8,128)(2,1)}) fusion(bf16[1,144,8,128]{3,2,1,0:T(8,128)(2,1)S(1)} %collective-permute-done.7, bf16[1,144,8,128]{3,2,1,0:T(8,128)(2,1)} %collective-permute-done.6, bf16[1,144,8,128]{3,2,1,0:T(8,128)(2,1)} %copy-done.9, ...), kind=kLoop, calls=%fused_computation.30 | loop fusion | flops 5308415 | bytes 3538945
  69.5 0.6 collective-permute-start.9
  70.1 2.4 %collective-permute-start.8 = (bf16[4,144,8,128]{3,2,1,0:T(8,128)(2,1)}, bf16[4,144,8,128]{3,2,1,0:T(8,128)(2,1)S(1)}, u32[]{:S(2)}, u32[]{:S(2)}) collective-permute-start(bf16[4,144,8,128]{3,2,1,0:T(8,128)(2,1)} %get-tuple-element.28.refs_3_), channel_id=1, source_target_pairs={{0,4},{2,6},{4,0},{6,2},{8,12},{10,14},{12,8},{14,10},{16,20},{18,... | collective-permute-start | bytes 3538952 | tf_op jit(solution)/shard_map/ppermute | solution.py:210
  72.5 22.0 %near_field.5 = (f32[24,16,256]{2,1,0:T(8,128)}, s32[1]{0:T(128)}) custom-call(s32[384]{0:T(512)} %reshape.51.refs_0_, bf16[136,16,256]{2,1,0:T(8,128)(2,1)} %pad_maximum_fusion.1.refs_1_, bf16[136,16,256]{2,1,0:T(8,128)(2,1)} %maximum_maximum_fusion.refs_2_, bf16[4,144,8,128]{3,2,1,0:T(8,128)(2,1)} %get-tuple-element.28.refs_3_), custom_call_target="tpu_custom_call" | custom-call | flops 603979776 | bytes 4194304 | tf_op jit(solution)/shard_map/near_field/pallas_call | solution.py:241
  95.3 1.5 collective-permute-done.9
  96.8 0.9 slice_select_fusion.1
  97.6 1.3 collective-permute-start.10
  99.0 0.9 slice_select_fusion.2.refs_3_
  99.8 1.7 collective-permute-start.11
  101.6 15.4 %near_field.6 = (f32[16,16,256]{2,1,0:T(8,128)}, s32[1]{0:T(128)}) custom-call(s32[384]{0:T(512)} %reshape.51.refs_0_, bf16[136,16,256]{2,1,0:T(8,128)(2,1)} %pad_maximum_fusion.1.refs_1_, bf16[136,16,256]{2,1,0:T(8,128)(2,1)} %maximum_maximum_fusion.refs_2_, bf16[2,144,8,128]{3,2,1,0:T(8,128)(2,1)} %slice_select_fusion.2.refs_3_), custom_call_target="tpu_custom_call" | custom-call | flops 402653184 | bytes 4194304 | tf_op jit(solution)/shard_map/near_field/pallas_call | solution.py:241
  117.6 0.2 constant_dynamic-update-slice_fusion.3
  117.8 0.2 constant_dynamic-update-slice_fusion.2
  118.1 1.1 constant_dynamic-update-slice_fusion
  119.3 2.1 %copy-done.1 = bf16[16,144,8,128]{3,2,1,0:T(8,128)(2,1)} copy-done((bf16[16,144,8,128]{3,2,1,0:T(8,128)(2,1)}, bf16[16,144,8,128]{3,2,1,0:T(8,128)(2,1)S(1)}, u32[]{:S(2)}) %copy-start.1) | copy-done | bytes 4718616
  121.4 0.1 slice_select_fusion
  121.6 0.1 copy.19
  121.8 0.1 reshape.66
  121.9 0.8 pad_maximum_fusion.2.refs_2_
  123.0 8.8 %near_field.7 = (f32[8,16,256]{2,1,0:T(8,128)}, s32[1]{0:T(128)}) custom-call(s32[384]{0:T(512)} %reshape.51.refs_0_, bf16[136,16,256]{2,1,0:T(8,128)(2,1)} %pad_maximum_fusion.1.refs_1_, bf16[136,16,256]{2,1,0:T(8,128)(2,1)} %maximum_maximum_fusion.refs_2_, bf16[768,8,128]{2,1,0:T(8,128)(2,1)} %bitcast.13), custom_call_target="tpu_custom_call" | custom-call | flops 201326592 | bytes 4194304 | tf_op jit(solution)/shard_map/near_field/pallas_call | solution.py:241
  131.8 0.9 constant_dynamic-update-slice_fusion.5
  132.8 0.9 fusion.18
  133.6 0.5 collective-permute-start.13
  134.2 0.1 reshape.64
  134.4 0.1 copy.17
  134.5 0.7 reshape.59.refs_0_
  135.3 0.1 reshape.58
  135.4 0.1 copy.20
  135.5 0.1 reshape.62
  135.6 0.1 copy.18
  135.7 0.7 reshape.50.refs_1_
  136.4 0.6 fusion.11.refs_0_
  137.0 3.9 %slice.108 = bf16[16,96,8,128]{3,2,1,0:T(8,128)(2,1)} slice(bf16[16,144,8,128]{3,2,1,0:T(8,128)(2,1)} %copy-done.1), slice={[0:16], [0:96], [0:8], [0:128]} | slice | bytes 6291456 | tf_op jit(solution)/shard_map/slice | solution.py:280
  141.0 7.3 %pad_maximum_fusion.refs_3_ = bf16[1536,8,128]{2,1,0:T(8,128)(2,1)} fusion(bf16[768,8,128]{2,1,0:T(8,128)(2,1)} %collective-permute-done.12, bf16[768,8,128]{2,1,0:T(8,128)(2,1)S(1)} %bitcast.14), kind=kLoop, calls=%fused_computation | loop fusion | flops 1572864 | bytes 6291456 | tf_op jit(solution)/shard_map/concatenate | solution.py:282
  148.3 16.7 %far_matrices.1.refs_2_ = bf16[192,64,512]{2,1,0:T(8,128)(2,1)} custom-call(s32[1536]{0:T(1024)} %fusion.11.refs_0_, s32[1536]{0:T(1024)} %reshape.50.refs_1_, bf16[192,8,64]{2,1,0:T(8,128)(2,1)} %pad_maximum_fusion.2.refs_2_, bf16[1536,8,128]{2,1,0:T(8,128)(2,1)} %pad_maximum_fusion.refs_3_), custom_call_target="tpu_custom_call" | custom-call | flops 402653184 | bytes 16777216 | tf_op jit(solution)/shard_map/far_matrices/pallas_call | solution.py:310
  164.9 13.0 %far_apply.1 = f32[192,8,64]{2,1,0:T(8,128)} custom-call(s32[1536]{0:T(1024)} %reshape.59.refs_0_, s32[1536]{0:T(1024)} %reshape.50.refs_1_, bf16[192,64,512]{2,1,0:T(8,128)(2,1)} %far_matrices.1.refs_2_, bf16[1536,8,128]{2,1,0:T(8,128)(2,1)} %bitcast.11), custom_call_target="tpu_custom_call" | custom-call | flops 100663296 | bytes 16777216 | tf_op jit(solution)/shard_map/far_apply/pallas_call | solution.py:322
  177.9 1.0 slice.123
  179.0 5.1 %fusion.1 = f32[128,8,256]{2,1,0:T(8,128)} fusion(f32[64,8,256]{2,1,0:T(8,128)S(1)} %collective-permute-done.13, f32[64,8,256]{2,1,0:T(8,128)S(1)} %get-tuple-element.29, pred[]{:T(512)S(6)} %eq.42, pred[128,256]{1,0:T(8,128)(4,1)S(1)} %iota_compare_fusion, bf16[128,64,256]{2,1,0:T(8,128)(2,1)} %basis_ref.1, f32[192,8,64]{2,1,0:T(8,128)} %far_apply.1, ...), kind=kOutput, calls=%fused_computation.7 | convolution fusion | flops 43384832 | bytes 8028161 | tf_op jit(solution)/shard_map/lck,lkp->lcp/dot_general | solution.py:340
  (65 shorter events, 0.8 us)
Async XLA Ops:
  4.7 26.7 %copy-start.7 = (bf16[64,8,64]{2,1,0:T(8,128)(2,1)S(1)}, bf16[64,8,64]{2,1,0:T(8,128)(2,1)}, u32[]{:S(2)}) copy-start(bf16[64,8,64]{2,1,0:T(8,128)(2,1)} %param.18) | copy-start | bytes 196612
  4.7 26.7 %copy-start.12 = (bf16[128,8,64]{0,2,1:T(8,128)(2,1)S(1)}, bf16[128,8,64]{0,2,1:T(8,128)(2,1)}, u32[]{:S(2)}) copy-start(bf16[128,8,64]{0,2,1:T(8,128)(2,1)} %param.17) | copy-start | bytes 393220
  16.7 26.5 %copy-start.4 = (bf16[128,16,256]{2,1,0:T(8,128)(2,1)S(1)}, bf16[128,16,256]{2,1,0:T(8,128)(2,1)}, u32[]{:S(2)}) copy-start(bf16[128,16,256]{2,1,0:T(8,128)(2,1)} %get-tuple-element.16) | copy-start | bytes 3145732
  16.7 29.1 %collective-permute-start.3 = (bf16[128,8,256]{2,1,0:T(8,128)(2,1)}, bf16[128,8,256]{2,1,0:T(8,128)(2,1)S(1)}, u32[]{:S(2)}, u32[]{:S(2)}) collective-permute-start(bf16[128,8,256]{2,1,0:T(8,128)(2,1)} %get-tuple-element.17), channel_id=1, source_target_pairs={{0,1},{1,0},{2,3},{3,2},{4,5},{5,4},{6,7},{7,6},{8,9},{9,8},{10,11... | collective-permute-start | bytes 1572872 | tf_op jit(solution)/shard_map/ppermute | solution.py:225
  17.9 24.7 %collective-permute-start.2 = (bf16[4,8,256]{2,1,0:T(8,128)(2,1)S(1)}, bf16[4,8,256]{2,1,0:T(8,128)(2,1)S(1)}, u32[]{:S(2)}, u32[]{:S(2)}) collective-permute-start(bf16[4,8,256]{2,1,0:T(8,128)(2,1)S(1)} %get-tuple-element.33), channel_id=1, source_target_pairs={{0,3},{1,2},{2,5},{3,4},{4,7},{5,6},{6,9},{7,8},{8,11},{9,10},{10,... | collective-permute-start | bytes 49160 | tf_op jit(solution)/shard_map/ppermute | solution.py:219
  22.4 23.3 %collective-permute-start.4 = (bf16[4,8,256]{2,1,0:T(8,128)(2,1)S(1)}, bf16[4,8,256]{2,1,0:T(8,128)(2,1)}, u32[]{:S(2)}, u32[]{:S(2)}) collective-permute-start(bf16[4,8,256]{2,1,0:T(8,128)(2,1)S(1)} %get-tuple-element.34), channel_id=1, source_target_pairs={{2,1},{3,0},{4,3},{5,2},{6,5},{7,4},{8,7},{9,6},{10,9},{11,8},{12,... | collective-permute-start | bytes 49160 | tf_op jit(solution)/shard_map/ppermute | solution.py:219
  24.5 11.2 %collective-permute-start.1 = (bf16[4,24,256]{2,1,0:T(8,128)(2,1)S(1)}, bf16[4,24,256]{2,1,0:T(8,128)(2,1)}, u32[]{:S(2)}, u32[]{:S(2)}) collective-permute-start(bf16[4,24,256]{2,1,0:T(8,128)(2,1)S(1)} %pad_maximum_fusion.4), channel_id=1, source_target_pairs={{2,0},{3,1},{4,2},{5,3},{6,4},{7,5},{8,6},{9,7},{10,8},{11,9},{12,... | collective-permute-start | bytes 147464 | tf_op jit(solution)/shard_map/ppermute | solution.py:219
  25.8 16.0 %collective-permute-start = (bf16[4,24,256]{2,1,0:T(8,128)(2,1)S(1)}, bf16[4,24,256]{2,1,0:T(8,128)(2,1)}, u32[]{:S(2)}, u32[]{:S(2)}) collective-permute-start(bf16[4,24,256]{2,1,0:T(8,128)(2,1)S(1)} %pad_maximum_fusion.3), channel_id=1, source_target_pairs={{0,2},{1,3},{2,4},{3,5},{4,6},{5,7},{6,8},{7,9},{8,10},{9,11},{10,... | collective-permute-start | bytes 147464 | tf_op jit(solution)/shard_map/ppermute | solution.py:219
  31.6 14.2 %copy-start.6 = (bf16[128,8,256]{2,1,0:T(8,128)(2,1)S(1)}, bf16[128,8,256]{2,1,0:T(8,128)(2,1)}, u32[]{:S(2)}) copy-start(bf16[128,8,256]{2,1,0:T(8,128)(2,1)} %get-tuple-element.17) | copy-start | bytes 1572868
  34.1 13.5 %copy-start.5 = (bf16[1,144,8,128]{3,2,1,0:T(8,128)(2,1)}, bf16[1,144,8,128]{3,2,1,0:T(8,128)(2,1)S(1)}, u32[]{:S(2)}) copy-start(bf16[1,144,8,128]{3,2,1,0:T(8,128)(2,1)S(1)} %maximum_bitcast_fusion.refs_3_) | copy-start | bytes 884740
  35.7 28.1 %collective-permute-start.7 = (bf16[1,144,8,128]{3,2,1,0:T(8,128)(2,1)S(1)}, bf16[1,144,8,128]{3,2,1,0:T(8,128)(2,1)S(1)}, u32[]{:S(2)}, u32[]{:S(2)}) collective-permute-start(bf16[1,144,8,128]{3,2,1,0:T(8,128)(2,1)S(1)} %maximum_bitcast_fusion.refs_3_), channel_id=1, source_target_pairs={{0,24},{2,26},{4,28},{6,30},{8,16},{10,18},{12,20},{14,22},{16,8},... | collective-permute-start | bytes 884744 | tf_op jit(solution)/shard_map/ppermute | solution.py:210
  41.8 24.5 %collective-permute-start.6 = (bf16[1,144,8,128]{3,2,1,0:T(8,128)(2,1)S(1)}, bf16[1,144,8,128]{3,2,1,0:T(8,128)(2,1)}, u32[]{:S(2)}, u32[]{:S(2)}) collective-permute-start(bf16[1,144,8,128]{3,2,1,0:T(8,128)(2,1)S(1)} %maximum_bitcast_fusion.refs_3_), channel_id=1, source_target_pairs={{0,16},{2,18},{4,20},{6,22},{8,24},{10,26},{12,28},{14,30},{16,0},... | collective-permute-start | bytes 884744 | tf_op jit(solution)/shard_map/ppermute | solution.py:210
  42.6 23.7 %collective-permute-start.5 = (bf16[1,144,8,128]{3,2,1,0:T(8,128)(2,1)S(1)}, bf16[1,144,8,128]{3,2,1,0:T(8,128)(2,1)S(1)}, u32[]{:S(2)}, u32[]{:S(2)}) collective-permute-start(bf16[1,144,8,128]{3,2,1,0:T(8,128)(2,1)S(1)} %maximum_bitcast_fusion.refs_3_), channel_id=1, source_target_pairs={{0,8},{2,10},{4,12},{6,14},{8,0},{10,2},{12,4},{14,6},{16,24},{18,... | collective-permute-start | bytes 884744 | tf_op jit(solution)/shard_map/ppermute | solution.py:210
  66.3 0.7 copy-start.9
  69.5 27.2 %collective-permute-start.9 = (bf16[4,144,8,128]{3,2,1,0:T(8,128)(2,1)}, bf16[4,144,8,128]{3,2,1,0:T(8,128)(2,1)S(1)}, u32[]{:S(2)}, u32[]{:S(2)}) collective-permute-start(bf16[4,144,8,128]{3,2,1,0:T(8,128)(2,1)} %get-tuple-element.28.refs_3_), channel_id=1, source_target_pairs={{0,2},{2,0},{4,6},{6,4},{8,10},{10,8},{12,14},{14,12},{16,18},{18,... | collective-permute-start | bytes 3538952 | tf_op jit(solution)/shard_map/ppermute | solution.py:210
  70.1 28.8 %collective-permute-start.8 = (bf16[4,144,8,128]{3,2,1,0:T(8,128)(2,1)}, bf16[4,144,8,128]{3,2,1,0:T(8,128)(2,1)S(1)}, u32[]{:S(2)}, u32[]{:S(2)}) collective-permute-start(bf16[4,144,8,128]{3,2,1,0:T(8,128)(2,1)} %get-tuple-element.28.refs_3_), channel_id=1, source_target_pairs={{0,4},{2,6},{4,0},{6,2},{8,12},{10,14},{12,8},{14,10},{16,20},{18,... | collective-permute-start | bytes 3538952 | tf_op jit(solution)/shard_map/ppermute | solution.py:210
  94.6 7.0 %copy-start.13 = (s32[128,8]{0,1:T(8,128)S(1)}, s32[128,8]{0,1:T(8,128)}, u32[]{:S(2)}) copy-start(s32[128,8]{0,1:T(8,128)} %param.21) | copy-start | bytes 12292
  97.6 20.3 %collective-permute-start.10 = (bf16[2,144,8,128]{3,2,1,0:T(8,128)(2,1)}, bf16[2,144,8,128]{3,2,1,0:T(8,128)(2,1)S(1)}, u32[]{:S(2)}, u32[]{:S(2)}) collective-permute-start(bf16[2,144,8,128]{3,2,1,0:T(8,128)(2,1)} %slice_select_fusion.1), channel_id=1, source_target_pairs={{0,4},{2,6},{4,0},{6,2},{8,12},{10,14},{12,8},{14,10},{16,20},{18,... | collective-permute-start | bytes 1769480 | tf_op jit(solution)/shard_map/ppermute | solution.py:210
  99.8 18.3 %collective-permute-start.11 = (bf16[2,144,8,128]{3,2,1,0:T(8,128)(2,1)}, bf16[2,144,8,128]{3,2,1,0:T(8,128)(2,1)}, u32[]{:S(2)}, u32[]{:S(2)}) collective-permute-start(bf16[2,144,8,128]{3,2,1,0:T(8,128)(2,1)} %slice_select_fusion.2.refs_3_), channel_id=1, source_target_pairs={{0,2},{2,0},{4,6},{6,4},{8,10},{10,8},{12,14},{14,12},{16,18},{18,... | collective-permute-start | bytes 1769480 | tf_op jit(solution)/shard_map/ppermute | solution.py:210
  118.1 3.5 %copy-start.14 = (s32[64,8]{0,1:T(8,128)S(1)}, s32[64,8]{0,1:T(8,128)}, u32[]{:S(2)}) copy-start(s32[64,8]{0,1:T(8,128)} %param.23) | copy-start | bytes 6148
  119.2 2.2 %copy-start.1 = (bf16[16,144,8,128]{3,2,1,0:T(8,128)(2,1)}, bf16[16,144,8,128]{3,2,1,0:T(8,128)(2,1)S(1)}, u32[]{:S(2)}) copy-start(bf16[16,144,8,128]{3,2,1,0:T(8,128)(2,1)S(1)} %constant_dynamic-update-slice_fusion) | copy-start | bytes 14155780
  119.2 3.5 %copy-start.17 = (s32[128]{0:T(128)S(1)}, s32[128]{0:T(128)}, u32[]{:S(2)}) copy-start(s32[128]{0:T(128)} %count_ref.1) | copy-start | bytes 1540
  119.3 3.6 %copy-start.10 = (f32[16,16,256]{2,1,0:T(8,128)S(1)}, f32[16,16,256]{2,1,0:T(8,128)}, u32[]{:S(2)}) copy-start(f32[16,16,256]{2,1,0:T(8,128)} %get-tuple-element.23) | copy-start | bytes 786436
  121.4 1.5 copy-start.8
  121.4 1.5 copy-start.11
  121.5 1.5 copy-start.2
  121.5 19.5 %collective-permute-start.12 = (bf16[768,8,128]{2,1,0:T(8,128)(2,1)S(1)}, bf16[768,8,128]{2,1,0:T(8,128)(2,1)}, u32[]{:S(2)}, u32[]{:S(2)}) collective-permute-start(bf16[768,8,128]{2,1,0:T(8,128)(2,1)S(1)} %bitcast.12), channel_id=1, source_target_pairs={{0,1},{1,0},{2,3},{3,2},{4,5},{5,4},{6,7},{7,6},{8,9},{9,8},{10,11... | collective-permute-start | bytes 4718600 | tf_op jit(solution)/shard_map/ppermute | solution.py:282
  131.8 2.3 %copy-start.15 = (s32[64,8]{0,1:T(8,128)S(1)}, s32[64,8]{0,1:T(8,128)}, u32[]{:S(2)}) copy-start(s32[64,8]{0,1:T(8,128)} %param.22) | copy-start | bytes 6148
  131.8 2.3 %copy-start.16 = (s32[128,8]{0,1:T(8,128)S(1)}, s32[128,8]{0,1:T(8,128)}, u32[]{:S(2)}) copy-start(s32[128,8]{0,1:T(8,128)} %param.20) | copy-start | bytes 12292
  133.6 45.3 %collective-permute-start.13 = (f32[64,8,256]{2,1,0:T(8,128)}, f32[64,8,256]{2,1,0:T(8,128)S(1)}, u32[]{:S(2)}, u32[]{:S(2)}) collective-permute-start(f32[64,8,256]{2,1,0:T(8,128)} %get-tuple-element.30), channel_id=1, source_target_pairs={{0,1},{1,0},{2,3},{3,2},{4,5},{5,4},{6,7},{7,6},{8,9},{9,8},{10,11... | collective-permute-start | bytes 1572872 | tf_op jit(solution)/shard_map/ppermute | solution.py:286
  137.0 4.0 %copy-start.3 = (bf16[16,48,8,128]{3,2,1,0:T(8,128)(2,1)S(1)}, bf16[16,48,8,128]{3,2,1,0:T(8,128)(2,1)}, u32[]{:S(2)}) copy-start(bf16[16,48,8,128]{3,2,1,0:T(8,128)(2,1)} %copy-done.2) | copy-start | bytes 4718596
  164.9 14.0 %copy-start = (bf16[128,64,64]{2,1,0:T(8,128)(2,1)S(1)}, bf16[128,64,64]{2,1,0:T(8,128)(2,1)}, u32[]{:S(2)}) copy-start(bf16[128,64,64]{2,1,0:T(8,128)(2,1)} %copy.25.transfer_ref) | copy-start | bytes 3145732

commit v2 on v1

--- a/solution.py
+++ b/solution.py
@@ -39,25 +39,14 @@
     return ((1.0 + dist * S_SCALE) * jnp.exp2(dist * EXP_SCALE)).astype(jnp.bfloat16)
 
 
-def prepare(count_ref, point_ref, value_ref, basis_ref, transfer_ref, feat_ref, masked_ref, coef_ref, upper_ref):
+def prepare(count_ref, point_ref, value_ref, feat_ref, masked_ref):
     leaves, columns, leaf_size = value_ref.shape
     base = pl.program_id(0) * leaves
     lane = lax.broadcasted_iota(jnp.int32, (columns, leaf_size), 1)
-    parent = None
     for u in range(leaves):
         feat_ref[u] = source_features(point_ref[u].astype(jnp.float32)).astype(jnp.bfloat16)
         kept = jnp.where(lane < count_ref[base + u], value_ref[u].astype(jnp.float32), 0.0)
-        kept = kept.astype(jnp.bfloat16)
-        masked_ref[u] = kept
-        coef = lax.dot_general(
-            kept, basis_ref[u], (((1,), (1,)), ((), ())), preferred_element_type=jnp.float32
-        ).astype(jnp.bfloat16)
-        coef_ref[u] = coef
-        term = jnp.dot(coef, transfer_ref[u], preferred_element_type=jnp.float32)
-        if u % 2 == 0:
-            parent = term
-        else:
-            upper_ref[u // 2] = (parent + term).astype(jnp.bfloat16)
+        masked_ref[u] = kept.astype(jnp.bfloat16)
 
 
 def near_kernel(near, offset, ids_ref, feat_ref, val_ref, _, out_ref, done_ref):
@@ -68,13 +57,13 @@
     def group(g, _):
         for u in range(pair):
             l = g * pair + u
-            base = (offset + l) * near
-            own = feat_ref[ids_ref[base]].astype(jnp.float32)
+            base = offset + l
+            own = feat_ref[ids_ref[base, 0]].astype(jnp.float32)
             target = jnp.concatenate([own[0:8] * -2.0, pltpu.roll(own[8:16], 4, 0)], axis=0)
             target = target.astype(jnp.bfloat16)
             total = None
             for j in range(near):
-                q = ids_ref[base + j]
+                q = ids_ref[base, j]
                 square = lax.dot_general(
                     feat_ref[q],
                     target,
@@ -89,22 +78,30 @@
     lax.fori_loop(0, leaves // pair, group, 0)
 
 
-def pick_pair(row_ref, half_ref, rows_ref, first, lane):
-    rank = rows_ref.shape[2] // 2
-    left = rows_ref[row_ref[first]].astype(jnp.float32)
-    right = rows_ref[row_ref[first + 1]].astype(jnp.float32)
-    left = pltpu.roll(left, half_ref[first] * rank, 1)
-    right = pltpu.roll(right, (1 - half_ref[first + 1]) * rank, 1)
+def side_by_side(left, left_half, right, right_half, lane):
+    rank = left.shape[1] // 2
+    left = pltpu.roll(left.astype(jnp.float32), left_half * rank, 1)
+    right = pltpu.roll(right.astype(jnp.float32), (1 - right_half) * rank, 1)
     return jnp.where(lane < rank, left, right)
 
 
-def far_kernel_matrix(far, row_ref, half_ref, target_ref, rows_ref, out_ref):
-    lane = lax.broadcasted_iota(jnp.int32, rows_ref.shape[1:], 1)
+def far_kernel_matrix(far, id_ref, target_ref, own_ref, other_ref, out_ref):
+    lane = lax.broadcasted_iota(jnp.int32, own_ref.shape[1:], 1)
+
+    def load(at):
+        word = id_ref[at]
+        own = own_ref[word >> 16]
+        other = other_ref[(word >> 2) & 0x3FFF]
+        return jnp.where((word & 2) == 2, own, other), word & 1
+
+    def pair(t, f):
+        return side_by_side(*load((t, f)), *load((t, f + 1)), lane)
+
     unroll = out_ref.shape[0]
     for u in range(unroll):
-        base = (pl.program_id(0) * unroll + u) * far
+        base = pl.program_id(0) * unroll + u
         sources = [
-            source_features(pick_pair(row_ref, half_ref, rows_ref, base + f, lane)).astype(jnp.bfloat16)
+            source_features(pair(base, f)).astype(jnp.bfloat16)
             for f in range(0, far, 2)
         ]
         target = target_features(target_ref[u].astype(jnp.float32)).T.astype(jnp.bfloat16)
@@ -114,13 +111,17 @@
         out_ref[u] = matern(square)
 
 
-def far_apply(far, row_ref, half_ref, matrix_ref, rows_ref, out_ref):
+def far_apply(far, id_ref, matrix_ref, rows_ref, out_ref):
     lane = lax.broadcasted_iota(jnp.int32, rows_ref.shape[1:], 1)
+
+    def load(at):
+        return rows_ref[id_ref[at] >> 1], id_ref[at] & 1
+
     unroll = out_ref.shape[0]
     for u in range(unroll):
-        base = (pl.program_id(0) * unroll + u) * far
+        base = pl.program_id(0) * unroll + u
         coefs = [
-            pick_pair(row_ref, half_ref, rows_ref, base + f, lane).astype(jnp.bfloat16)
+            side_by_side(*load((base, f)), *load((base, f + 1)), lane).astype(jnp.bfloat16)
             for f in range(0, far, 2)
         ]
         out_ref[u] = lax.dot_general(
@@ -167,32 +168,35 @@
     vmem = pl.BlockSpec(memory_space=pltpu.VMEM)
     params = pltpu.CompilerParams(vmem_limit_bytes=VMEM)
 
-    group = math.gcd(leaf_dev, UNROLL)
-    feats, masked, leaf_coef, upper_coef = pl.pallas_call(
+    group = math.gcd(leaf_dev, 2 * UNROLL)
+    feats, masked = pl.pallas_call(
         prepare,
         grid=(leaf_dev // group,),
         in_specs=[
             smem,
             pl.BlockSpec((group, 8, leaf_size), lambda g: (g, 0, 0)),
             pl.BlockSpec((group, columns, leaf_size), lambda g: (g, 0, 0)),
-            pl.BlockSpec((group, rank, leaf_size), lambda g: (g, 0, 0)),
-            pl.BlockSpec((group, rank, rank), lambda g: (g, 0, 0)),
         ],
         out_specs=[
             pl.BlockSpec((group, 16, leaf_size), lambda g: (g, 0, 0)),
             pl.BlockSpec((group, columns, leaf_size), lambda g: (g, 0, 0)),
-            pl.BlockSpec((group, columns, rank), lambda g: (g, 0, 0)),
-            pl.BlockSpec((group // 2, columns, rank), lambda g: (g, 0, 0)),
         ],
         out_shape=[
             jax.ShapeDtypeStruct((leaf_dev, 16, leaf_size), jnp.bfloat16),
             jax.ShapeDtypeStruct((leaf_dev, columns, leaf_size), jnp.bfloat16),
-            jax.ShapeDtypeStruct((leaf_dev, columns, rank), jnp.bfloat16),
-            jax.ShapeDtypeStruct((par_dev, columns, rank), jnp.bfloat16),
         ],
         compiler_params=params,
         name="prepare",
-    )(counts, points, values, leaf_basis, transfer)
+    )(counts, points, values)
+    leaf_coef = jnp.einsum(
+        "lcp,lkp->lck", masked, leaf_basis, preferred_element_type=jnp.float32
+    ).astype(jnp.bfloat16)
+    upper_coef = jnp.einsum(
+        "pjck,pjkm->pcm",
+        leaf_coef.reshape(par_dev, 2, columns, rank),
+        transfer.reshape(par_dev, 2, rank, rank),
+        preferred_element_type=jnp.float32,
+    ).astype(jnp.bfloat16)
 
     skeletons = jnp.concatenate([paired(leaf_skeleton), paired(upper_skeleton)], axis=0)
     piece = block // 2
@@ -231,7 +235,7 @@
 
     first_leaf = me * leaf_dev - HALO
     start = side * half
-    near_ids = (lax.dynamic_slice_in_dim(near_list, start, half) - first_leaf).reshape(-1)
+    near_ids = lax.dynamic_slice_in_dim(near_list, start, half) - first_leaf
 
     def after_piece(done, cells):
         return jnp.where(done[0] == 0, cells, jnp.zeros_like(cells))
@@ -277,9 +281,9 @@
 
         def position(owner):
             return owner
-    coefs = everything[:, :block].reshape(count * block, columns, 2 * rank)
     half_skel = after_piece(done, everything[:, block:]).reshape(count * piece, 8, 2 * rank)
-    skeletons = jnp.concatenate([half_skel, lax.ppermute(half_skel, "rhs", swap)], axis=0)
+    other_skel = lax.ppermute(half_skel, "rhs", swap)
+    everything = everything.reshape(count * (block + piece), 8, 2 * rank)
     near3, _ = near_piece(cuts[3], sizes[3], half_skel)
     near_half = jnp.concatenate([near0, near1, near2, near3], axis=0)
     mine = near_half[:, :columns]
@@ -292,17 +296,15 @@
     live = lax.broadcasted_iota(jnp.int32, (leaf_dev, leaf_size), 1) < counts[:, None]
 
     targets = jnp.concatenate([leaf_skeleton, upper_skeleton], axis=0)
-    row_in_block = jnp.concatenate(
-        [far_local % half, half + upper_local % upper_half], axis=0
-    ).reshape(-1)
-    place = position(jnp.concatenate([far_owner, upper_owner], axis=0).reshape(-1))
-    row_ids = place * block + row_in_block
-    skel_ids = (
-        jnp.where(row_in_block // piece == side, 0, count * piece)
-        + place * piece
-        + row_in_block % piece
-    )
-    half_ids = jnp.concatenate([far_local // half, upper_local // upper_half], axis=0).reshape(-1)
+    row_in_block = jnp.concatenate([far_local % half, half + upper_local % upper_half], axis=0)
+    place = position(jnp.concatenate([far_owner, upper_owner], axis=0))
+    row_ids = place * (block + piece) + row_in_block
+    own_ids = place * (block + piece) + block + row_in_block % piece
+    other_ids = place * piece + row_in_block % piece
+    own_flags = jnp.where(row_in_block // piece == side, 1, 0)
+    half_ids = jnp.concatenate([far_local // half, upper_local // upper_half], axis=0)
+    skel_ids = (own_ids << 16) + (other_ids << 2) + (own_flags << 1) + half_ids
+    coef_ids = row_ids * 2 + half_ids
     clusters = leaf_dev + par_dev
     unroll = math.gcd(clusters, UNROLL)
     pairs_far = clusters * far * rank * rank
@@ -311,26 +313,26 @@
         lambda *refs: far_kernel_matrix(far, *refs),
         grid=(clusters // unroll,),
         out_shape=jax.ShapeDtypeStruct((clusters, rank, far * rank), jnp.bfloat16),
-        in_specs=[smem, smem, pl.BlockSpec((unroll, 8, rank), lambda g: (g, 0, 0)), vmem],
+        in_specs=[smem, pl.BlockSpec((unroll, 8, rank), lambda g: (g, 0, 0)), vmem, vmem],
         out_specs=matrix_spec,
         compiler_params=params,
         cost_estimate=pl.CostEstimate(
             flops=pairs_far * 64, bytes_accessed=1 << 24, transcendentals=pairs_far * 2
         ),
         name="far_matrices",
-    )(skel_ids, half_ids, targets, skeletons)
+    )(skel_ids, targets, everything, other_skel)
     field = pl.pallas_call(
         lambda *refs: far_apply(far, *refs),
         grid=(clusters // unroll,),
         out_shape=jax.ShapeDtypeStruct((clusters, columns, rank), jnp.float32),
-        in_specs=[smem, smem, matrix_spec, vmem],
+        in_specs=[smem, matrix_spec, vmem],
         out_specs=pl.BlockSpec((unroll, columns, rank), lambda g: (g, 0, 0)),
         compiler_params=params,
         cost_estimate=pl.CostEstimate(
             flops=pairs_far * 16, bytes_accessed=1 << 24, transcendentals=0
         ),
         name="far_apply",
-    )(row_ids, half_ids, matrix, coefs)
+    )(coef_ids, matrix, everything)
 
     spread = jnp.repeat(field[leaf_dev:].astype(jnp.bfloat16), 2, axis=0)
     leaf_field = (

time: 185 us -> 187 us (1.011)
  Pallas kernels: 104 us -> 98.9 us
  matrix products: 5.07 us -> 9.37 us
    pallas_call x1, Pallas kernels: 12 us -> 3.84 us  [body(): pl.pallas_call(prepare, grid=(leaf_dev // group,), in_specs=[smem, pl.Blo...]
    concatenate x1, other arithmetic: 7.3 us -> 0.01 us  [body(): place = position(jnp.concatenate([far_owner, upper_owner], axis=0))]
    dot_general x0 -> x2, matrix products: none -> 4.24 us  [the longest x1 3.54 us: body(): jnp.einsum('lcp,lkp->lck', masked, leaf_basis, preferred_element_type=jnp...]
    slice x1 -> x0, local copies, waits for them, and re-layouts: 3.94 us -> none  [body(): coefs = everything[:, :block].reshape(count * block, columns, 2 * rank)]
    unnamed x44 -> x41, local copies, waits for them, and re-layouts: 8.22 us -> 11.5 us
    pallas_call x1, Pallas kernels: 16.7 us -> 19.8 us  [body(): pl.pallas_call(lambda *refs: far_kernel_matrix(far, *refs), grid=(cluster...]
    select_n x3, other arithmetic: 1.81 us -> 4.11 us  [after_piece(): return jnp.where(done[0] == 0, cells, jnp.zeros_like(cells))]
  transfers between devices with their start and end apart: 14 -> 14, of which waited for: 2 -> 2; matrix products, arithmetic and copies ran while one was open for 17% -> 23% of each run, Pallas kernels for 50% -> 51%
where the time goes in v2:
time: 187 us; the launch traced here: 186 us
  Pallas kernels  98.9 us (53%)
  local copies, waits for them, and re-layouts  25.9 us (14%)
  starting transfers between devices  25.5 us (14%)
  other arithmetic  18.2 us (10%)
  matrix products  9.37 us (5%)
  waiting for transfers between devices  5.4 us (3%)
  between operations  2.28 us (1%)
    pallas_call x4, Pallas kernels, near_piece(): pl.pallas_call(lambda *refs: near_kernel(near, offset, *refs), out_shape=...  61.8 us
    pallas_call x1, Pallas kernels, body(): pl.pallas_call(lambda *refs: far_kernel_matrix(far, *refs), grid=(cluster...  19.8 us
    pallas_call x1, Pallas kernels, body(): pl.pallas_call(lambda *refs: far_apply(far, *refs), grid=(clusters // unr...  13.5 us
    ppermute x4, starting transfers between devices, shifted(): return lax.ppermute(cells, ('leaf', 'rhs'), pairs)  13 us
    unnamed x41, local copies, waits for them, and re-layouts  11.5 us
    ppermute x7, starting transfers between devices, across(): return lax.ppermute(cells, 'leaf', [(i, i ^ bits) for i in range(count)])  11.4 us
    ppermute x7, waiting for transfers between devices, across(): return lax.ppermute(cells, 'leaf', [(i, i ^ bits) for i in range(count)])  5.38 us
    dot_general x1, matrix products, body(): jnp.einsum('lck,lkp->lcp', leaf_field, leaf_basis, preferred_element_type...  5.13 us
  transfers between devices with their start and end apart: 14, of which 2 were waited for; matrix products, arithmetic and copies ran while one was open for 23% of the time, Pallas kernels for 51%

profile of v2, /device:TPU:0, one launch (start us, length us, event | category | flops | bytes accessed | tf_op | source)
XLA Modules:
  0.0 185.5 jit_solution(1398498639359229188)
XLA Ops:
  0.0 3.8 %prepare.1 = (bf16[128,16,256]{2,1,0:T(8,128)(2,1)}, bf16[128,8,256]{2,1,0:T(8,128)(2,1)}) custom-call(s32[128]{0:T(128)} %count_ref.1, bf16[128,8,256]{2,1,0:T(8,128)(2,1)} %point_ref.1, bf16[128,8,256]{2,1,0:T(8,128)(2,1)} %value_ref.1), custom_call_target="tpu_custom_call" | custom-call | tf_op jit(solution)/shard_map/prepare/pallas_call | solution.py:172
  3.8 0.5 collective-permute-start.3
  4.3 1.4 fusion.19
  5.7 5.1 %collective-permute-start.2 = (bf16[4,8,256]{2,1,0:T(8,128)(2,1)}, bf16[4,8,256]{2,1,0:T(8,128)(2,1)}, u32[]{:S(2)}, u32[]{:S(2)}) collective-permute-start(bf16[4,8,256]{2,1,0:T(8,128)(2,1)} %get-tuple-element.29), channel_id=1, source_target_pairs={{0,3},{1,2},{2,5},{3,4},{4,7},{5,6},{6,9},{7,8},{8,11},{9,10},{10,... | collective-permute-start | bytes 49160 | tf_op jit(solution)/shard_map/ppermute | solution.py:223
  10.7 1.3 collective-permute-start.4
  12.0 0.8 fusion.18
  12.8 1.3 pad_maximum_fusion.3
  14.2 1.3 collective-permute-start.1
  15.4 1.3 pad_maximum_fusion.2
  16.8 5.4 %collective-permute-start = (bf16[4,24,256]{2,1,0:T(8,128)(2,1)}, bf16[4,24,256]{2,1,0:T(8,128)(2,1)}, u32[]{:S(2)}, u32[]{:S(2)}) collective-permute-start(bf16[4,24,256]{2,1,0:T(8,128)(2,1)} %pad_maximum_fusion.2), channel_id=1, source_target_pairs={{0,2},{1,3},{2,4},{3,5},{4,6},{5,7},{6,8},{7,9},{8,10},{9,11},{10,... | collective-permute-start | bytes 147464 | tf_op jit(solution)/shard_map/ppermute | solution.py:223
  22.3 0.7 copy.76
  23.0 1.5 fusion.23
  24.5 1.1 copy.69
  25.6 3.5 %convolution_convert_fusion = bf16[128,8,64]{2,1,0:T(8,128)(2,1)S(1)} fusion(bf16[128,8,256]{2,1,0:T(8,128)(2,1)} %get-tuple-element.15, bf16[128,64,256]{2,1,0:T(8,128)(2,1)} %param.15), kind=kOutput, calls=%fused_computation.1 | convolution fusion | flops 33619968 | bytes 4849664 | tf_op jit(solution)/shard_map/lcp,lkp->lck/dot_general | solution.py:191
  29.1 3.9 %copy.71 = bf16[128,64,64]{2,1,0:T(8,128)(2,1)S(1)} copy(bf16[128,64,64]{0,2,1:T(8,128)(2,1)} %param.16) | data formatting | bytes 2097152 | tf_op args[4]
  33.1 0.7 fusion
  33.8 1.5 broadcast_subtract_fusion.refs_0_
  35.3 0.2 fusion.9
  35.6 0.1 maximum_bitcast_fusion.refs_3_
  35.7 4.8 %collective-permute-start.7 = (bf16[1,144,8,128]{3,2,1,0:T(8,128)(2,1)S(1)}, bf16[1,144,8,128]{3,2,1,0:T(8,128)(2,1)S(1)}, u32[]{:S(2)}, u32[]{:S(2)}) collective-permute-start(bf16[1,144,8,128]{3,2,1,0:T(8,128)(2,1)S(1)} %maximum_bitcast_fusion.refs_3_), channel_id=1, source_target_pairs={{0,24},{2,26},{4,28},{6,30},{8,16},{10,18},{12,20},{14,22},{16,8},... | collective-permute-start | bytes 884744 | tf_op jit(solution)/shard_map/ppermute | solution.py:214
  40.6 0.8 slice.96
  41.3 0.8 slice.95
  42.1 0.6 collective-permute-start.5
  42.7 1.2 pad_maximum_fusion.refs_1_
  43.8 0.7 slice.98
  44.6 0.7 slice.97
  45.3 2.1 %maximum_maximum_fusion.refs_2_ = bf16[136,16,256]{2,1,0:T(8,128)(2,1)} fusion(bf16[4,8,256]{2,1,0:T(8,128)(2,1)} %collective-permute-done.4, bf16[128,8,256]{2,1,0:T(8,128)(2,1)} %collective-permute-done.3, bf16[4,8,256]{2,1,0:T(8,128)(2,1)} %collective-permute-done.2, bf16[4,8,256]{2,1,0:T(8,128)(2,1)S(1)} %slice.98, bf16[128,8,256]{2,1,0:T(8,128)(2,1)S(1)} %copy-done.2, ...), kind=kLoop, calls=%fused_computation.6 | loop fusion | flops 6684672 | bytes 2228224 | tf_op jit(solution)/shard_map/concatenate | solution.py:234
  47.4 15.4 %near_field.4 = (f32[16,16,256]{2,1,0:T(8,128)}, s32[1]{0:T(128)}) custom-call(s32[64,6]{1,0:T(8,128)} %broadcast_subtract_fusion.refs_0_, bf16[136,16,256]{2,1,0:T(8,128)(2,1)} %pad_maximum_fusion.refs_1_, bf16[136,16,256]{2,1,0:T(8,128)(2,1)} %maximum_maximum_fusion.refs_2_, bf16[1,144,8,128]{3,2,1,0:T(8,128)(2,1)} %copy-done.4), custom_call_target="tpu_custom_call" | custom-call | flops 402653184 | bytes 4194304 | tf_op jit(solution)/shard_map/near_field/pallas_call | solution.py:245
  63.5 3.1 %collective-permute-done.6 = bf16[1,144,8,128]{3,2,1,0:T(8,128)(2,1)S(1)} collective-permute-done((bf16[1,144,8,128]{3,2,1,0:T(8,128)(2,1)S(1)}, bf16[1,144,8,128]{3,2,1,0:T(8,128)(2,1)S(1)}, u32[]{:S(2)}, u32[]{:S(2)}) %collective-permute-start.6) | collective-permute-done | bytes 294944 | tf_op jit(solution)/shard_map/ppermute | solution.py:214
  66.7 0.7 copy-done.7
  67.4 2.4 %constant_dynamic-update-slice_fusion.4 = (bf16[16,144,8,128]{3,2,1,0:T(8,128)(2,1)S(1)}, bf16[4,144,8,128]{3,2,1,0:T(8,128)(2,1)}) fusion(bf16[1,144,8,128]{3,2,1,0:T(8,128)(2,1)S(1)} %collective-permute-done.7, bf16[1,144,8,128]{3,2,1,0:T(8,128)(2,1)S(1)} %collective-permute-done.6, bf16[1,144,8,128]{3,2,1,0:T(8,128)(2,1)} %copy-done.7, ...), kind=kLoop, calls=%fused_computation.40 | loop fusion | flops 5308415 | bytes 3538945
  69.8 0.6 collective-permute-start.8
  70.4 2.4 %collective-permute-start.9 = (bf16[4,144,8,128]{3,2,1,0:T(8,128)(2,1)}, bf16[4,144,8,128]{3,2,1,0:T(8,128)(2,1)}, u32[]{:S(2)}, u32[]{:S(2)}) collective-permute-start(bf16[4,144,8,128]{3,2,1,0:T(8,128)(2,1)} %get-tuple-element.24.refs_3_), channel_id=1, source_target_pairs={{0,4},{2,6},{4,0},{6,2},{8,12},{10,14},{12,8},{14,10},{16,20},{18,... | collective-permute-start | bytes 3538952 | tf_op jit(solution)/shard_map/ppermute | solution.py:214
  72.8 22.1 %near_field.5 = (f32[24,16,256]{2,1,0:T(8,128)}, s32[1]{0:T(128)}) custom-call(s32[64,6]{1,0:T(8,128)} %broadcast_subtract_fusion.refs_0_, bf16[136,16,256]{2,1,0:T(8,128)(2,1)} %pad_maximum_fusion.refs_1_, bf16[136,16,256]{2,1,0:T(8,128)(2,1)} %maximum_maximum_fusion.refs_2_, bf16[4,144,8,128]{3,2,1,0:T(8,128)(2,1)} %get-tuple-element.24.refs_3_), custom_call_target="tpu_custom_call" | custom-call | flops 603979776 | bytes 4194304 | tf_op jit(solution)/shard_map/near_field/pallas_call | solution.py:245
  95.5 2.3 %collective-permute-done.8 = bf16[4,144,8,128]{3,2,1,0:T(8,128)(2,1)S(1)} collective-permute-done((bf16[4,144,8,128]{3,2,1,0:T(8,128)(2,1)}, bf16[4,144,8,128]{3,2,1,0:T(8,128)(2,1)S(1)}, u32[]{:S(2)}, u32[]{:S(2)}) %collective-permute-start.8) | collective-permute-done | bytes 1179680 | tf_op jit(solution)/shard_map/ppermute | solution.py:214
  97.8 0.9 slice_select_fusion.2
  98.7 1.3 collective-permute-start.10
  100.0 1.9 %slice_select_fusion.1.refs_3_ = bf16[2,144,8,128]{3,2,1,0:T(8,128)(2,1)} fusion(bf16[4,144,8,128]{3,2,1,0:T(8,128)(2,1)} %collective-permute-done.9, pred[]{:T(512)} %bitcast.6), kind=kLoop, calls=%fused_computation.10 | loop fusion | flops 294912 | bytes 1179649 | tf_op jit(solution)/shard_map/jit(_where)/select_n | solution.py:241
  101.9 1.7 collective-permute-start.11
  103.6 15.4 %near_field.6 = (f32[16,16,256]{2,1,0:T(8,128)}, s32[1]{0:T(128)}) custom-call(s32[64,6]{1,0:T(8,128)} %broadcast_subtract_fusion.refs_0_, bf16[136,16,256]{2,1,0:T(8,128)(2,1)} %pad_maximum_fusion.refs_1_, bf16[136,16,256]{2,1,0:T(8,128)(2,1)} %maximum_maximum_fusion.refs_2_, bf16[2,144,8,128]{3,2,1,0:T(8,128)(2,1)} %slice_select_fusion.1.refs_3_), custom_call_target="tpu_custom_call" | custom-call | flops 402653184 | bytes 4194304 | tf_op jit(solution)/shard_map/near_field/pallas_call | solution.py:245
  119.7 0.2 constant_dynamic-update-slice_fusion.3
  119.9 1.4 constant_dynamic-update-slice_fusion.2
  121.3 1.1 constant_dynamic-update-slice_fusion.1
  122.5 1.2 constant_dynamic-update-slice_fusion
  123.7 1.3 slice_select_fusion
  125.0 0.6 broadcast_divide_fusion
  125.6 0.8 pad_maximum_fusion.1.refs_1_
  126.4 0.7 constant_dynamic-update-slice_fusion.8
  127.2 0.8 constant_dynamic-update-slice_fusion.7
  127.9 0.7 constant_dynamic-update-slice_fusion.6
  128.7 8.8 %near_field.7 = (f32[8,16,256]{2,1,0:T(8,128)}, s32[1]{0:T(128)}) custom-call(s32[64,6]{1,0:T(8,128)} %broadcast_subtract_fusion.refs_0_, bf16[136,16,256]{2,1,0:T(8,128)(2,1)} %pad_maximum_fusion.refs_1_, bf16[136,16,256]{2,1,0:T(8,128)(2,1)} %maximum_maximum_fusion.refs_2_, bf16[768,8,128]{2,1,0:T(8,128)(2,1)} %bitcast.9.refs_3_), custom_call_target="tpu_custom_call" | custom-call | flops 201326592 | bytes 4194304 | tf_op jit(solution)/shard_map/near_field/pallas_call | solution.py:245
  137.5 1.6 constant_dynamic-update-slice_fusion.5
  139.1 2.1 %fusion.17 = (f32[64,8,256]{2,1,0:T(8,128)S(1)}, f32[64,8,256]{2,1,0:T(8,128)}) fusion(f32[64,16,256]{2,1,0:T(8,128)} %constant_dynamic-update-slice_fusion.5), kind=kLoop, calls=%fused_computation.69 | loop fusion | bytes 2097152 | tf_op jit(solution)/shard_map/slice | solution.py:289
  141.2 0.5 collective-permute-start.13
  141.8 0.1 copy.59
  141.9 0.1 copy.66
  142.1 0.8 copy.61
  142.9 0.8 copy.62
  143.6 0.7 iota_compare_fusion
  144.3 1.7 add_add_fusion
  146.1 19.8 %far_matrices.1.refs_1_ = bf16[192,64,512]{2,1,0:T(8,128)(2,1)} custom-call(s32[192,8]{1,0:T(8,128)} %get-tuple-element.31.refs_0_, bf16[192,8,64]{2,1,0:T(8,128)(2,1)} %pad_maximum_fusion.1.refs_1_, bf16[2304,8,128]{2,1,0:T(8,128)(2,1)} %bitcast.23, bf16[768,8,128]{2,1,0:T(8,128)(2,1)} %collective-permute-done.12.refs_3_), custom_call_target="tpu_custom_call" | custom-call | flops 402653184 | bytes 16777216 | tf_op jit(solution)/shard_map/far_matrices/pallas_call | solution.py:312
  165.9 13.5 %far_apply.1 = f32[192,8,64]{2,1,0:T(8,128)} custom-call(s32[192,8]{1,0:T(8,128)} %get-tuple-element.32.refs_0_, bf16[192,64,512]{2,1,0:T(8,128)(2,1)} %far_matrices.1.refs_1_, bf16[2304,8,128]{2,1,0:T(8,128)(2,1)} %bitcast.24), custom_call_target="tpu_custom_call" | custom-call | flops 100663296 | bytes 16777216 | tf_op jit(solution)/shard_map/far_apply/pallas_call | solution.py:324
  179.3 1.0 slice.122
  180.4 5.1 %fusion.2 = f32[128,8,256]{2,1,0:T(8,128)} fusion(f32[64,8,256]{2,1,0:T(8,128)S(1)} %collective-permute-done.13, f32[64,8,256]{2,1,0:T(8,128)S(1)} %get-tuple-element.25, pred[]{:T(512)S(6)} %eq.43, pred[128,256]{1,0:T(8,128)(4,1)S(1)} %copy-done.10, bf16[128,64,256]{2,1,0:T(8,128)(2,1)} %param.15, f32[192,8,64]{2,1,0:T(8,128)} %far_apply.1, ...), kind=kOutput, calls=%fused_computation.9 | convolution fusion | flops 43384832 | bytes 8028161 | tf_op jit(solution)/shard_map/lck,lkp->lcp/dot_general | solution.py:342
  (54 shorter events, 0.4 us)
Async XLA Ops:
  0.0 22.2 %copy-start = (s32[128,6]{0,1:T(8,128)S(1)}, s32[128,6]{0,1:T(8,128)}, u32[]{:S(2)}) copy-start(s32[128,6]{0,1:T(8,128)} %param.19) | copy-start | bytes 9220
  3.8 41.4 %collective-permute-start.3 = (bf16[128,8,256]{2,1,0:T(8,128)(2,1)}, bf16[128,8,256]{2,1,0:T(8,128)(2,1)}, u32[]{:S(2)}, u32[]{:S(2)}) collective-permute-start(bf16[128,8,256]{2,1,0:T(8,128)(2,1)} %get-tuple-element.15), channel_id=1, source_target_pairs={{0,1},{1,0},{2,3},{3,2},{4,5},{5,4},{6,7},{7,6},{8,9},{9,8},{10,11... | collective-permute-start | bytes 1572872 | tf_op jit(solution)/shard_map/ppermute | solution.py:229
  5.7 36.4 %collective-permute-start.2 = (bf16[4,8,256]{2,1,0:T(8,128)(2,1)}, bf16[4,8,256]{2,1,0:T(8,128)(2,1)}, u32[]{:S(2)}, u32[]{:S(2)}) collective-permute-start(bf16[4,8,256]{2,1,0:T(8,128)(2,1)} %get-tuple-element.29), channel_id=1, source_target_pairs={{0,3},{1,2},{2,5},{3,4},{4,7},{5,6},{6,9},{7,8},{8,11},{9,10},{10,... | collective-permute-start | bytes 49160 | tf_op jit(solution)/shard_map/ppermute | solution.py:223
  10.7 34.5 %collective-permute-start.4 = (bf16[4,8,256]{2,1,0:T(8,128)(2,1)}, bf16[4,8,256]{2,1,0:T(8,128)(2,1)}, u32[]{:S(2)}, u32[]{:S(2)}) collective-permute-start(bf16[4,8,256]{2,1,0:T(8,128)(2,1)} %get-tuple-element.30), channel_id=1, source_target_pairs={{2,1},{3,0},{4,3},{5,2},{6,5},{7,4},{8,7},{9,6},{10,9},{11,8},{12,... | collective-permute-start | bytes 49160 | tf_op jit(solution)/shard_map/ppermute | solution.py:223
  14.2 21.6 %collective-permute-start.1 = (bf16[4,24,256]{2,1,0:T(8,128)(2,1)}, bf16[4,24,256]{2,1,0:T(8,128)(2,1)}, u32[]{:S(2)}, u32[]{:S(2)}) collective-permute-start(bf16[4,24,256]{2,1,0:T(8,128)(2,1)} %pad_maximum_fusion.3), channel_id=1, source_target_pairs={{2,0},{3,1},{4,2},{5,3},{6,4},{7,5},{8,6},{9,7},{10,8},{11,9},{12,... | collective-permute-start | bytes 147464 | tf_op jit(solution)/shard_map/ppermute | solution.py:223
  16.8 24.5 %collective-permute-start = (bf16[4,24,256]{2,1,0:T(8,128)(2,1)}, bf16[4,24,256]{2,1,0:T(8,128)(2,1)}, u32[]{:S(2)}, u32[]{:S(2)}) collective-permute-start(bf16[4,24,256]{2,1,0:T(8,128)(2,1)} %pad_maximum_fusion.2), channel_id=1, source_target_pairs={{0,2},{1,3},{2,4},{3,5},{4,6},{5,7},{6,8},{7,9},{8,10},{9,11},{10,... | collective-permute-start | bytes 147464 | tf_op jit(solution)/shard_map/ppermute | solution.py:223
  33.8 11.5 %copy-start.2 = (bf16[128,8,256]{2,1,0:T(8,128)(2,1)S(1)}, bf16[128,8,256]{2,1,0:T(8,128)(2,1)}, u32[]{:S(2)}) copy-start(bf16[128,8,256]{2,1,0:T(8,128)(2,1)} %get-tuple-element.15) | copy-start | bytes 1572868
  33.8 8.9 %copy-start.3 = (bf16[128,16,256]{2,1,0:T(8,128)(2,1)S(1)}, bf16[128,16,256]{2,1,0:T(8,128)(2,1)}, u32[]{:S(2)}) copy-start(bf16[128,16,256]{2,1,0:T(8,128)(2,1)} %get-tuple-element.14) | copy-start | bytes 3145732
  35.7 11.7 %copy-start.4 = (bf16[1,144,8,128]{3,2,1,0:T(8,128)(2,1)}, bf16[1,144,8,128]{3,2,1,0:T(8,128)(2,1)S(1)}, u32[]{:S(2)}) copy-start(bf16[1,144,8,128]{3,2,1,0:T(8,128)(2,1)S(1)} %maximum_bitcast_fusion.refs_3_) | copy-start | bytes 884740
  35.7 27.8 %collective-permute-start.7 = (bf16[1,144,8,128]{3,2,1,0:T(8,128)(2,1)S(1)}, bf16[1,144,8,128]{3,2,1,0:T(8,128)(2,1)S(1)}, u32[]{:S(2)}, u32[]{:S(2)}) collective-permute-start(bf16[1,144,8,128]{3,2,1,0:T(8,128)(2,1)S(1)} %maximum_bitcast_fusion.refs_3_), channel_id=1, source_target_pairs={{0,24},{2,26},{4,28},{6,30},{8,16},{10,18},{12,20},{14,22},{16,8},... | collective-permute-start | bytes 884744 | tf_op jit(solution)/shard_map/ppermute | solution.py:214
  41.3 25.3 %collective-permute-start.6 = (bf16[1,144,8,128]{3,2,1,0:T(8,128)(2,1)S(1)}, bf16[1,144,8,128]{3,2,1,0:T(8,128)(2,1)S(1)}, u32[]{:S(2)}, u32[]{:S(2)}) collective-permute-start(bf16[1,144,8,128]{3,2,1,0:T(8,128)(2,1)S(1)} %maximum_bitcast_fusion.refs_3_), channel_id=1, source_target_pairs={{0,16},{2,18},{4,20},{6,22},{8,24},{10,26},{12,28},{14,30},{16,0},... | collective-permute-start | bytes 884744 | tf_op jit(solution)/shard_map/ppermute | solution.py:214
  42.1 24.6 %collective-permute-start.5 = (bf16[1,144,8,128]{3,2,1,0:T(8,128)(2,1)S(1)}, bf16[1,144,8,128]{3,2,1,0:T(8,128)(2,1)S(1)}, u32[]{:S(2)}, u32[]{:S(2)}) collective-permute-start(bf16[1,144,8,128]{3,2,1,0:T(8,128)(2,1)S(1)} %maximum_bitcast_fusion.refs_3_), channel_id=1, source_target_pairs={{0,8},{2,10},{4,12},{6,14},{8,0},{10,2},{12,4},{14,6},{16,24},{18,... | collective-permute-start | bytes 884744 | tf_op jit(solution)/shard_map/ppermute | solution.py:214
  66.7 0.7 copy-start.7
  69.8 28.0 %collective-permute-start.8 = (bf16[4,144,8,128]{3,2,1,0:T(8,128)(2,1)}, bf16[4,144,8,128]{3,2,1,0:T(8,128)(2,1)S(1)}, u32[]{:S(2)}, u32[]{:S(2)}) collective-permute-start(bf16[4,144,8,128]{3,2,1,0:T(8,128)(2,1)} %get-tuple-element.24.refs_3_), channel_id=1, source_target_pairs={{0,2},{2,0},{4,6},{6,4},{8,10},{10,8},{12,14},{14,12},{16,18},{18,... | collective-permute-start | bytes 3538952 | tf_op jit(solution)/shard_map/ppermute | solution.py:214
  70.4 29.6 %collective-permute-start.9 = (bf16[4,144,8,128]{3,2,1,0:T(8,128)(2,1)}, bf16[4,144,8,128]{3,2,1,0:T(8,128)(2,1)}, u32[]{:S(2)}, u32[]{:S(2)}) collective-permute-start(bf16[4,144,8,128]{3,2,1,0:T(8,128)(2,1)} %get-tuple-element.24.refs_3_), channel_id=1, source_target_pairs={{0,4},{2,6},{4,0},{6,2},{8,12},{10,14},{12,8},{14,10},{16,20},{18,... | collective-permute-start | bytes 3538952 | tf_op jit(solution)/shard_map/ppermute | solution.py:214
  94.9 8.8 %copy-start.11 = (s32[128,8]{0,1:T(8,128)S(1)}, s32[128,8]{0,1:T(8,128)}, u32[]{:S(2)}) copy-start(s32[128,8]{0,1:T(8,128)} %param.21) | copy-start | bytes 12292
  98.7 22.6 %collective-permute-start.10 = (bf16[2,144,8,128]{3,2,1,0:T(8,128)(2,1)}, bf16[2,144,8,128]{3,2,1,0:T(8,128)(2,1)}, u32[]{:S(2)}, u32[]{:S(2)}) collective-permute-start(bf16[2,144,8,128]{3,2,1,0:T(8,128)(2,1)} %slice_select_fusion.2), channel_id=1, source_target_pairs={{0,4},{2,6},{4,0},{6,2},{8,12},{10,14},{12,8},{14,10},{16,20},{18,... | collective-permute-start | bytes 1769480 | tf_op jit(solution)/shard_map/ppermute | solution.py:214
  101.9 20.6 %collective-permute-start.11 = (bf16[2,144,8,128]{3,2,1,0:T(8,128)(2,1)}, bf16[2,144,8,128]{3,2,1,0:T(8,128)(2,1)}, u32[]{:S(2)}, u32[]{:S(2)}) collective-permute-start(bf16[2,144,8,128]{3,2,1,0:T(8,128)(2,1)} %slice_select_fusion.1.refs_3_), channel_id=1, source_target_pairs={{0,2},{2,0},{4,6},{6,4},{8,10},{10,8},{12,14},{14,12},{16,18},{18,... | collective-permute-start | bytes 1769480 | tf_op jit(solution)/shard_map/ppermute | solution.py:214
  122.5 2.6 %copy-start.12 = (s32[64,8]{0,1:T(8,128)S(1)}, s32[64,8]{0,1:T(8,128)}, u32[]{:S(2)}) copy-start(s32[64,8]{0,1:T(8,128)} %param.23) | copy-start | bytes 6148
  122.5 3.2 %copy-start.5 = (bf16[64,8,64]{2,1,0:T(8,128)(2,1)S(1)}, bf16[64,8,64]{2,1,0:T(8,128)(2,1)}, u32[]{:S(2)}) copy-start(bf16[64,8,64]{2,1,0:T(8,128)(2,1)} %param.18) | copy-start | bytes 196612
  123.7 13.8 %copy-start.1 = (bf16[16,144,8,128]{3,2,1,0:T(8,128)(2,1)}, bf16[16,144,8,128]{3,2,1,0:T(8,128)(2,1)S(1)}, u32[]{:S(2)}) copy-start(bf16[16,144,8,128]{3,2,1,0:T(8,128)(2,1)S(1)} %constant_dynamic-update-slice_fusion) | copy-start | bytes 14155780
  123.7 2.8 %copy-start.8 = (f32[16,16,256]{2,1,0:T(8,128)S(1)}, f32[16,16,256]{2,1,0:T(8,128)}, u32[]{:S(2)}) copy-start(f32[16,16,256]{2,1,0:T(8,128)} %get-tuple-element.19) | copy-start | bytes 786436
  123.7 3.5 %copy-start.6 = (f32[24,16,256]{2,1,0:T(8,128)S(1)}, f32[24,16,256]{2,1,0:T(8,128)}, u32[]{:S(2)}) copy-start(f32[24,16,256]{2,1,0:T(8,128)} %get-tuple-element.20) | copy-start | bytes 1179652
  123.7 4.2 %copy-start.9 = (f32[16,16,256]{2,1,0:T(8,128)S(1)}, f32[16,16,256]{2,1,0:T(8,128)}, u32[]{:S(2)}) copy-start(f32[16,16,256]{2,1,0:T(8,128)} %get-tuple-element.21) | copy-start | bytes 786436
  125.0 21.1 %collective-permute-start.12 = (bf16[768,8,128]{2,1,0:T(8,128)(2,1)}, bf16[768,8,128]{2,1,0:T(8,128)(2,1)}, u32[]{:S(2)}, u32[]{:S(2)}) collective-permute-start(bf16[768,8,128]{2,1,0:T(8,128)(2,1)} %bitcast.9.refs_3_), channel_id=1, source_target_pairs={{0,1},{1,0},{2,3},{3,2},{4,5},{5,4},{6,7},{7,6},{8,9},{9,8},{10,11... | collective-permute-start | bytes 4718600 | tf_op jit(solution)/shard_map/ppermute | solution.py:285
  137.5 4.2 %copy-start.13 = (s32[64,8]{0,1:T(8,128)S(1)}, s32[64,8]{0,1:T(8,128)}, u32[]{:S(2)}) copy-start(s32[64,8]{0,1:T(8,128)} %param.22) | copy-start | bytes 6148
  137.5 4.2 %copy-start.14 = (s32[128,8]{0,1:T(8,128)S(1)}, s32[128,8]{0,1:T(8,128)}, u32[]{:S(2)}) copy-start(s32[128,8]{0,1:T(8,128)} %param.20) | copy-start | bytes 12292
  137.5 6.1 %copy-start.15 = (s32[128]{0:T(128)S(1)}, s32[128]{0:T(128)}, u32[]{:S(2)}) copy-start(s32[128]{0:T(128)} %count_ref.1) | copy-start | bytes 1540
  141.2 39.1 %collective-permute-start.13 = (f32[64,8,256]{2,1,0:T(8,128)}, f32[64,8,256]{2,1,0:T(8,128)S(1)}, u32[]{:S(2)}, u32[]{:S(2)}) collective-permute-start(f32[64,8,256]{2,1,0:T(8,128)} %get-tuple-element.26), channel_id=1, source_target_pairs={{0,1},{1,0},{2,3},{3,2},{4,5},{5,4},{6,7},{7,6},{8,9},{9,8},{10,11... | collective-permute-start | bytes 1572872 | tf_op jit(solution)/shard_map/ppermute | solution.py:290
  165.9 14.5 %copy-start.10 = (pred[128,256]{1,0:T(8,128)(4,1)S(1)}, pred[128,256]{1,0:T(8,128)(4,1)}, u32[]{:S(2)}) copy-start(pred[128,256]{1,0:T(8,128)(4,1)} %iota_compare_fusion) | copy-start | bytes 98308

commit v3 on v2

v3 whole, which is shorter than its diff:
```python
import math

import jax
import jax.numpy as jnp
from jax import lax
from jax.experimental import pallas as pl
from jax.experimental.pallas import tpu as pltpu
from jax.sharding import PartitionSpec as P

HALO = 4
ROWS = 64
UNROLL = 16
S_SCALE = math.sqrt(3.0) / 1.5
EXP_SCALE = -S_SCALE / math.log(2.0)
TINY = 1e-12
VMEM = 56 * 1024 * 1024


def norm_rows(coords):
    row = lax.broadcasted_iota(jnp.int32, coords.shape, 0)
    norm = jnp.sum(coords * coords, axis=0, keepdims=True)
    high = norm.astype(jnp.bfloat16).astype(jnp.float32)
    rest = norm - high
    mid = rest.astype(jnp.bfloat16).astype(jnp.float32)
    ones = jnp.where((row >= 4) & (row < 7), 1.0, 0.0)
    return jnp.where(row == 0, high, jnp.where(row == 1, mid, jnp.where(row == 2, rest - mid, ones)))


def source_features(coords):
    return jnp.concatenate([coords, norm_rows(coords)], axis=0)


def target_features(coords):
    return jnp.concatenate([coords * -2.0, pltpu.roll(norm_rows(coords), 4, 0)], axis=0)


def matern(square):
    bounded = jnp.maximum(square, TINY)
    dist = bounded * lax.rsqrt(bounded)
    return ((1.0 + dist * S_SCALE) * jnp.exp2(dist * EXP_SCALE)).astype(jnp.bfloat16)


def near_kernel(near, ids_ref, point_ref, val_ref, out_ref, done_ref, source_ref):
    done_ref[0] = 0
    sources = point_ref.shape[0]
    leaves = out_ref.shape[0]
    wide = math.gcd(sources, 8)
    pair = math.gcd(leaves, 2)

    def turn(g, _):
        for u in range(wide):
            q = g * wide + u
            rows = source_features(point_ref[q].astype(jnp.float32))
            source_ref[q] = rows.T.astype(jnp.bfloat16)
        return 0

    lax.fori_loop(0, sources // wide, turn, 0)

    def group(g, _):
        for u in range(pair):
            l = g * pair + u
            own = point_ref[ids_ref[l, 0]].astype(jnp.float32)
            target = target_features(own).astype(jnp.bfloat16)
            total = None
            for j in range(near):
                q = ids_ref[l, j]
                blocks = [
                    matern(
                        jnp.dot(
                            source_ref[q, r : r + ROWS], target, preferred_element_type=jnp.float32
                        )
                    )
                    for r in range(0, source_ref.shape[1], ROWS)
                ]
                part = jnp.dot(
                    val_ref[q], jnp.concatenate(blocks, axis=0), preferred_element_type=jnp.float32
                )
                total = part if total is None else total + part
            out_ref[l] = total
        return 0

    lax.fori_loop(0, leaves // pair, group, 0)


def side_by_side(left, left_half, right, right_half, lane):
    rank = left.shape[1] // 2
    left = pltpu.roll(left.astype(jnp.float32), left_half * rank, 1)
    right = pltpu.roll(right.astype(jnp.float32), (1 - right_half) * rank, 1)
    return jnp.where(lane < rank, left, right)


def far_kernel_matrix(far, id_ref, target_ref, own_ref, other_ref, out_ref):
    lane = lax.broadcasted_iota(jnp.int32, own_ref.shape[1:], 1)

    def load(at):
        word = id_ref[at]
        own = own_ref[word >> 16]
        other = other_ref[(word >> 2) & 0x3FFF]
        return jnp.where((word & 2) == 2, own, other), word & 1

    def pair(t, f):
        return side_by_side(*load((t, f)), *load((t, f + 1)), lane)

    unroll = out_ref.shape[0]
    for u in range(unroll):
        base = pl.program_id(0) * unroll + u
        sources = [
            source_features(pair(base, f)).astype(jnp.bfloat16)
            for f in range(0, far, 2)
        ]
        target = target_features(target_ref[u].astype(jnp.float32)).T.astype(jnp.bfloat16)
        square = jnp.dot(
            target, jnp.concatenate(sources, axis=1), preferred_element_type=jnp.float32
        )
        out_ref[u] = matern(square)


def far_apply(far, id_ref, matrix_ref, rows_ref, out_ref):
    lane = lax.broadcasted_iota(jnp.int32, rows_ref.shape[1:], 1)

    def load(at):
        return rows_ref[id_ref[at] >> 1], id_ref[at] & 1

    unroll = out_ref.shape[0]
    for u in range(unroll):
        base = pl.program_id(0) * unroll + u
        coefs = [
            side_by_side(*load((base, f)), *load((base, f + 1)), lane).astype(jnp.bfloat16)
            for f in range(0, far, 2)
        ]
        out_ref[u] = lax.dot_general(
            jnp.concatenate(coefs, axis=1),
            matrix_ref[u],
            (((1,), (1,)), ((), ())),
            preferred_element_type=jnp.float32,
        )


def paired(bundle):
    half = bundle.shape[0] // 2
    return jnp.concatenate([bundle[:half], bundle[half:]], axis=2)


def body(
    points,
    values,
    counts,
    leaf_basis,
    transfer,
    leaf_skeleton,
    upper_skeleton,
    near_list,
    far_owner,
    far_local,
    upper_owner,
    upper_local,
):
    leaf_dev, _, leaf_size = points.shape
    columns = values.shape[1]
    rank = leaf_basis.shape[1]
    far = far_owner.shape[1]
    near = near_list.shape[1]
    par_dev = leaf_dev // 2
    half = leaf_dev // 2
    upper_half = par_dev // 2
    block = half + upper_half
    count = lax.axis_size("leaf")
    side = lax.axis_index("rhs")
    swap = [(0, 1), (1, 0)]

    live = lax.broadcasted_iota(jnp.int32, (leaf_dev, leaf_size), 1) < counts[:, None]
    masked = jnp.where(live[:, None, :], values, jnp.zeros_like(values))

    def shifted(cells, step):
        if step > 0:
            pairs = [(i, i + 1) for i in range(count - 1)]
            return lax.ppermute(cells[leaf_dev - HALO :], "leaf", pairs)
        pairs = [(i + 1, i) for i in range(count - 1)]
        return lax.ppermute(cells[:HALO], "leaf", pairs)

    bundle = jnp.concatenate([points, masked], axis=1)
    extended = jnp.concatenate([shifted(bundle, 1), bundle, shifted(bundle, -1)], axis=0)
    own_vals = extended[:, 8:]
    vals = jnp.concatenate([own_vals, lax.ppermute(own_vals, "rhs", swap)], axis=1)

    leaf_coef = jnp.einsum(
        "lcp,lkp->lck", masked, leaf_basis, preferred_element_type=jnp.float32
    ).astype(jnp.bfloat16)
    upper_coef = jnp.einsum(
        "pjck,pjkm->pcm",
        leaf_coef.reshape(par_dev, 2, columns, rank),
        transfer.reshape(par_dev, 2, rank, rank),
        preferred_element_type=jnp.float32,
    ).astype(jnp.bfloat16)
    skeletons = jnp.concatenate([paired(leaf_skeleton), paired(upper_skeleton)], axis=0)
    piece = block // 2
    packed = jnp.concatenate(
        [
            paired(leaf_coef),
            paired(upper_coef),
            lax.dynamic_slice_in_dim(skeletons, side * piece, piece),
        ],
        axis=0,
    )
    everything = lax.all_gather(packed, "leaf", axis=0, tiled=True)
    first_leaf = lax.axis_index("leaf") * leaf_dev - HALO
    start = side * half
    near_ids = (lax.dynamic_slice_in_dim(near_list, start, half) - first_leaf)
    smem = pl.BlockSpec(memory_space=pltpu.SMEM)
    vmem = pl.BlockSpec(memory_space=pltpu.VMEM)
    pairs_near = half * near * leaf_size * leaf_size
    near_half, done = pl.pallas_call(
        lambda *refs: near_kernel(near, *refs),
        out_shape=[
            jax.ShapeDtypeStruct((half, 2 * columns, leaf_size), jnp.float32),
            jax.ShapeDtypeStruct((1,), jnp.int32),
        ],
        in_specs=[smem, vmem, vmem],
        out_specs=[vmem, smem],
        scratch_shapes=[pltpu.VMEM((leaf_dev + 2 * HALO, leaf_size, 16), jnp.bfloat16)],
        compiler_params=pltpu.CompilerParams(vmem_limit_bytes=VMEM),
        cost_estimate=pl.CostEstimate(
            flops=pairs_near * 64, bytes_accessed=1 << 22, transcendentals=pairs_near * 2
        ),
        name="near_field",
    )(near_ids, extended[:, :8], vals)
    own_skel = everything.reshape(count, block + piece, 8, 2 * rank)[:, block:]
    own_skel = jnp.where(done[0] == 0, own_skel, jnp.zeros_like(own_skel))
    other_skel = lax.ppermute(own_skel, "rhs", swap).reshape(count * piece, 8, 2 * rank)
    mine = near_half[:, :columns]
    other = lax.ppermute(near_half[:, columns:], "rhs", swap)
    near_part = jnp.where(
        side == 0,
        jnp.concatenate([mine, other], axis=0),
        jnp.concatenate([other, mine], axis=0),
    )

    targets = jnp.concatenate([leaf_skeleton, upper_skeleton], axis=0)
    row_in_block = jnp.concatenate([far_local % half, half + upper_local % upper_half], axis=0)
    place = jnp.concatenate([far_owner, upper_owner], axis=0)
    row_ids = place * (block + piece) + row_in_block
    own_ids = place * (block + piece) + block + row_in_block % piece
    other_ids = place * piece + row_in_block % piece
    own_flags = jnp.where(row_in_block // piece == side, 1, 0)
    half_ids = jnp.concatenate([far_local // half, upper_local // upper_half], axis=0)
    skel_ids = (own_ids << 16) + (other_ids << 2) + (own_flags << 1) + half_ids
    coef_ids = row_ids * 2 + half_ids
    clusters = leaf_dev + par_dev
    unroll = math.gcd(clusters, UNROLL)
    pairs_far = clusters * far * rank * rank
    params = pltpu.CompilerParams(vmem_limit_bytes=VMEM)
    matrix_spec = pl.BlockSpec((unroll, rank, far * rank), lambda g: (g, 0, 0))
    matrix = pl.pallas_call(
        lambda *refs: far_kernel_matrix(far, *refs),
        grid=(clusters // unroll,),
        out_shape=jax.ShapeDtypeStruct((clusters, rank, far * rank), jnp.bfloat16),
        in_specs=[smem, pl.BlockSpec((unroll, 8, rank), lambda g: (g, 0, 0)), vmem, vmem],
        out_specs=matrix_spec,
        compiler_params=params,
        cost_estimate=pl.CostEstimate(
            flops=pairs_far * 64, bytes_accessed=1 << 24, transcendentals=pairs_far * 2
        ),
        name="far_matrices",
    )(skel_ids, targets, everything, other_skel)
    field = pl.pallas_call(
        lambda *refs: far_apply(far, *refs),
        grid=(clusters // unroll,),
        out_shape=jax.ShapeDtypeStruct((clusters, columns, rank), jnp.float32),
        in_specs=[smem, matrix_spec, vmem],
        out_specs=pl.BlockSpec((unroll, columns, rank), lambda g: (g, 0, 0)),
        compiler_params=params,
        cost_estimate=pl.CostEstimate(
            flops=pairs_far * 16, bytes_accessed=1 << 24, transcendentals=0
        ),
        name="far_apply",
    )(coef_ids, matrix, everything)

    spread = jnp.repeat(field[leaf_dev:].astype(jnp.bfloat16), 2, axis=0)
    leaf_field = (
        field[:leaf_dev]
        + jnp.einsum("lcm,lkm->lck", spread, transfer, preferred_element_type=jnp.float32)
    ).astype(jnp.bfloat16)
    far_part = jnp.einsum(
        "lck,lkp->lcp", leaf_field, leaf_basis, preferred_element_type=jnp.float32
    )
    return jnp.where(live[:, None, :], far_part + near_part, 0.0)


def solution(mesh):
    return jax.shard_map(
        body,
        mesh=mesh,
        in_specs=(
            P("leaf", None, None),
            P("leaf", "rhs", None),
            P("leaf"),
            P("leaf", None, None),
            P("leaf", None, None),
            P("leaf", None, None),
            P("leaf", None, None),
            P("leaf", None),
            P("leaf", None),
            P("leaf", None),
            P("leaf", None),
            P("leaf", None),
        ),
        out_specs=P("leaf", "rhs", None),
        check_vma=False,
    )
```

time: 187 us -> 178 us (0.952)
  starting transfers between devices: 25.5 us -> 6.65 us
  between operations: 2.28 us -> 14.2 us
  Pallas kernels: 98.9 us -> 106 us
  other arithmetic: 18.2 us -> 13.5 us
  local copies, waits for them, and re-layouts: 25.9 us -> 21.5 us
    ppermute x13 -> x4, starting transfers between devices: 24.9 us -> 6.25 us  [the longest x1 4.84 us: shifted(): return lax.ppermute(cells[leaf_dev - HALO:], 'leaf', pairs)]
    pallas_call x5 -> x1, Pallas kernels: 65.6 us -> 72.7 us  [body(): pl.pallas_call(lambda *refs: near_kernel(near, *refs), out_shape=[jax.Sha...]
    unnamed x41 -> x22, local copies, waits for them, and re-layouts: 11.5 us -> 5.17 us
    slice x6 -> x1, local copies, waits for them, and re-layouts: 5.1 us -> 0.87 us  [body(): own_vals = extended[:, 8:]]
    concatenate x5 -> x3, other arithmetic: 5.98 us -> 3.06 us  [the longest x1 1.89 us: body(): jnp.concatenate([paired(leaf_coef), paired(upper_coef), lax.dynamic_slice...]
    concatenate x3 -> x1, local copies, waits for them, and re-layouts: 2.87 us -> 0.01 us  [body(): place = jnp.concatenate([far_owner, upper_owner], axis=0)]
    unnamed x1 -> x0, other arithmetic: 2.39 us -> none
    mul x0 -> x2, local copies, waits for them, and re-layouts: none -> 2.2 us  [the longest x1 1.45 us: body(): other_ids = place * piece + row_in_block % piece]
  transfers between devices with their start and end apart: 14 -> 6, of which waited for: 2 -> 3; matrix products, arithmetic and copies ran while one was open for 23% -> 11% of each run, Pallas kernels for 51% -> 60%
where the time goes in v3:
time: 178 us; the launch traced here: 177 us
  Pallas kernels  106 us (60%)
  local copies, waits for them, and re-layouts  21.5 us (12%)
  between operations  14.2 us (8%)
  other arithmetic  13.5 us (8%)
  matrix products  9.2 us (5%)
  starting transfers between devices  6.65 us (4%)
  waiting for transfers between devices  5.72 us (3%)
    pallas_call x1, Pallas kernels, body(): pl.pallas_call(lambda *refs: near_kernel(near, *refs), out_shape=[jax.Sha...  72.7 us
    pallas_call x1, Pallas kernels, body(): pl.pallas_call(lambda *refs: far_kernel_matrix(far, *refs), grid=(cluster...  19.8 us
    pallas_call x1, Pallas kernels, body(): pl.pallas_call(lambda *refs: far_apply(far, *refs), grid=(clusters // unr...  13.5 us
    unnamed x22, local copies, waits for them, and re-layouts  5.17 us
    dot_general x1, matrix products, body(): jnp.einsum('lck,lkp->lcp', leaf_field, leaf_basis, preferred_element_type...  5.13 us
    ppermute x1, starting transfers between devices, shifted(): return lax.ppermute(cells[leaf_dev - HALO:], 'leaf', pairs)  4.84 us
    ppermute x1, waiting for transfers between devices, shifted(): return lax.ppermute(cells[:HALO], 'leaf', pairs)  4.23 us
    slice x4, local copies, waits for them, and re-layouts, paired(): return jnp.concatenate([bundle[:half], bundle[half:]], axis=2)  3.61 us
  transfers between devices with their start and end apart: 6, of which 3 were waited for; matrix products, arithmetic and copies ran while one was open for 11% of the time, Pallas kernels for 60%

profile of v3, /device:TPU:0, one launch (start us, length us, event | category | flops | bytes accessed | tf_op | source)
XLA Modules:
  0.0 176.7 jit_solution(16714508686476665866)
XLA Ops:
  6.5 0.0 copy-start
  6.5 0.0 all-gather.2.cloned.1.call-start
  6.5 0.7 iota_compare_fusion
  7.3 0.0 copy-start.3
  7.3 1.5 fusion.22
  8.9 1.1 copy.76
  9.9 0.7 fusion.20
  10.6 0.0 copy-done.3
  10.6 1.2 broadcast_select_fusion
  11.8 3.4 %convolution_convert_fusion = bf16[128,8,64]{2,1,0:T(8,128)(2,1)S(1)} fusion(bf16[128,8,256]{2,1,0:T(8,128)(2,1)S(1)} %broadcast_select_fusion, bf16[128,64,256]{2,1,0:T(8,128)(2,1)} %param.15), kind=kOutput, calls=%fused_computation.1 | convolution fusion | flops 33619968 | bytes 4849664 | tf_op jit(solution)/shard_map/lcp,lkp->lck/dot_general | solution.py:186
  15.2 0.7 fusion.19
  15.9 3.9 %copy.77 = bf16[128,64,64]{2,1,0:T(8,128)(2,1)S(1)} copy(bf16[128,64,64]{0,2,1:T(8,128)(2,1)} %param.16) | data formatting | bytes 2097152 | tf_op args[4]
  19.9 0.7 fusion
  20.6 0.7 fusion.21
  21.2 1.1 fusion.9
  22.3 1.9 %pad_maximum_fusion.3 = bf16[144,8,128]{2,1,0:T(8,128)(2,1)} fusion(bf16[48,8,128]{2,1,0:T(8,128)(2,1)S(1)} %fusion.9, bf16[32,8,64]{2,1,0:T(8,128)(2,1)} %get-tuple-element.22, bf16[32,8,64]{2,1,0:T(8,128)(2,1)} %get-tuple-element.21, bf16[64,8,64]{2,1,0:T(8,128)(2,1)} %get-tuple-element.16, bf16[64,8,64]{2,1,0:T(8,128)(2,1)} %get-tuple-element.15), kind=kLoop, calls=%fused_computation.13 | loop fusion | flops 1474560 | bytes 589824 | tf_op jit(solution)/shard_map/concatenate | solution.py:197
  24.2 0.0 all-gather.2.cloned.1.call-update
  24.3 0.0 copy-done.1
  24.3 4.8 %collective-permute-start = (bf16[4,16,256]{2,1,0:T(8,128)(2,1)S(1)}, bf16[4,16,256]{2,1,0:T(8,128)(2,1)S(1)}, u32[]{:S(2)}, u32[]{:S(2)}) collective-permute-start(bf16[4,16,256]{2,1,0:T(8,128)(2,1)S(1)} %get-tuple-element.13), channel_id=1, source_target_pairs={{0,2},{2,4},{4,6},{6,8},{8,10},{10,12},{12,14},{14,16},{16,18},{18... | collective-permute-start | bytes 98312 | tf_op jit(solution)/shard_map/ppermute | solution.py:177
  29.1 1.3 collective-permute-start.1
  30.4 0.3 collective-permute-done
  30.7 4.2 %collective-permute-done.1 = bf16[4,16,256]{2,1,0:T(8,128)(2,1)S(1)} collective-permute-done((bf16[4,16,256]{2,1,0:T(8,128)(2,1)S(1)}, bf16[4,16,256]{2,1,0:T(8,128)(2,1)S(1)}, u32[]{:S(2)}, u32[]{:S(2)}) %collective-permute-start.1) | collective-permute-done | bytes 32800 | tf_op jit(solution)/shard_map/ppermute | solution.py:179
  34.9 0.1 pad_maximum_fusion
  35.0 0.9 fusion.17
  35.9 0.0 collective-permute-start.2
  35.9 0.0 copy-done
  35.9 0.1 constant_dynamic-slice_fusion
  36.0 0.1 copy.83
  36.1 0.6 broadcast_subtract_fusion.refs_0_
  36.7 1.2 collective-permute-done.2
  37.9 1.1 pad_maximum_fusion.1.refs_2_
  39.0 72.7 %near_field.1 = (f32[64,16,256]{2,1,0:T(8,128)}, s32[1]{0:T(128)}) custom-call(s32[64,6]{1,0:T(8,128)} %broadcast_subtract_fusion.refs_0_, bf16[136,8,256]{2,1,0:T(8,128)(2,1)} %get-tuple-element.10.refs_1_, bf16[136,16,256]{2,1,0:T(8,128)(2,1)} %pad_maximum_fusion.1.refs_2_), custom_call_target="tpu_custom_call" | custom-call | flops 1610612736 | bytes 4194304 | tf_op jit(solution)/shard_map/near_field/pallas_call | solution.py:212
  111.7 0.0 copy-start.7
  111.7 0.0 copy-start.8
  111.7 0.0 copy-start.5
  111.7 0.0 copy-start.6
  112.3 0.0 all-gather.2.cloned.1.call-done.refs_2_
  112.3 2.7 %slice_select_fusion = bf16[16,48,8,128]{3,2,1,0:T(8,128)(2,1)} fusion(bf16[16,144,8,128]{3,2,1,0:T(8,128)(2,1)} %bitcast.19, pred[]{:T(512)} %bitcast.4), kind=kLoop, calls=%fused_computation | loop fusion | flops 786432 | bytes 3145729 | tf_op jit(solution)/shard_map/jit(_where)/select_n | solution.py:228
  115.1 0.1 collective-permute-start.3
  115.2 0.0 copy-done.7
  115.2 0.0 copy-done.8
  115.2 0.6 broadcast_add_fusion.1
  115.8 0.8 copy.70
  116.5 0.0 copy-done.5
  116.5 0.0 copy-done.6
  116.6 2.1 %fusion.18 = (f32[64,8,256]{2,1,0:T(8,128)S(1)}, f32[64,8,256]{2,1,0:T(8,128)}) fusion(f32[64,16,256]{2,1,0:T(8,128)} %get-tuple-element.8), kind=kLoop, calls=%fused_computation.62 | loop fusion | bytes 2097152 | tf_op jit(solution)/shard_map/slice | solution.py:230
  118.6 0.4 collective-permute-start.4
  119.0 0.6 broadcast_divide_fusion
  119.7 1.4 copy.74
  121.1 1.4 copy.71
  122.6 0.8 copy.64
  123.3 1.4 copy.73
  124.8 1.4 copy.65
  126.2 1.4 copy.66
  127.6 0.0 copy-done.2
  127.6 0.8 pad_maximum_fusion.2.refs_1_
  128.5 2.0 %add_add_fusion = (s32[192,8]{1,0:T(8,128)}, s32[192,8]{1,0:T(8,128)}) fusion(s32[192,8]{1,0:T(8,128)} %copy.66, s32[192,8]{1,0:T(8,128)} %copy.71, s32[192,8]{1,0:T(8,128)} %copy.70, s32[192,8]{1,0:T(8,128)} %copy.73, s32[192,8]{1,0:T(8,128)} %copy.74, s32[192,8]{1,0:T(8,128)} %copy.65, s32[]{:T(128)S(6)} %axis_index.22, s32[192,8]{1,0:T(8,128)} %copy.64), kind=kLoop, calls=%fused_computation.25 | loop fusion | flops 35328 | bytes 55300 | tf_op jit(solution)/shard_map/add | solution.py:246
  130.5 0.0 collective-permute-done.3
  130.5 19.8 %far_matrices.1.refs_1_ = bf16[192,64,512]{2,1,0:T(8,128)(2,1)} custom-call(s32[192,8]{1,0:T(8,128)} %get-tuple-element.19.refs_0_, bf16[192,8,64]{2,1,0:T(8,128)(2,1)} %pad_maximum_fusion.2.refs_1_, bf16[2304,8,128]{2,1,0:T(8,128)(2,1)} %all-gather.2.cloned.1.call-done.refs_2_, bf16[768,8,128]{2,1,0:T(8,128)(2,1)} %bitcast.6.refs_3_), custom_call_target="tpu_custom_call" | custom-call | flops 402653184 | bytes 16777216 | tf_op jit(solution)/shard_map/far_matrices/pallas_call | solution.py:253
  150.2 13.5 %far_apply.1 = f32[192,8,64]{2,1,0:T(8,128)} custom-call(s32[192,8]{1,0:T(8,128)} %get-tuple-element.20.refs_0_, bf16[192,64,512]{2,1,0:T(8,128)(2,1)} %far_matrices.1.refs_1_, bf16[2304,8,128]{2,1,0:T(8,128)(2,1)} %all-gather.2.cloned.1.call-done.refs_2_), custom_call_target="tpu_custom_call" | custom-call | flops 100663296 | bytes 16777216 | tf_op jit(solution)/shard_map/far_apply/pallas_call | solution.py:265
  163.7 1.0 slice.88
  164.7 0.0 collective-permute-done.4
  164.7 0.0 copy-done.4
  164.7 5.1 %fusion.2 = f32[128,8,256]{2,1,0:T(8,128)} fusion(f32[64,8,256]{2,1,0:T(8,128)S(1)} %collective-permute-done.4, f32[64,8,256]{2,1,0:T(8,128)S(1)} %get-tuple-element.11, pred[]{:T(512)S(6)} %eq.26, pred[128,256]{1,0:T(8,128)(4,1)S(1)} %copy-done.4, bf16[128,64,256]{2,1,0:T(8,128)(2,1)} %param.15, f32[192,8,64]{2,1,0:T(8,128)} %far_apply.1, ...), kind=kOutput, calls=%fused_computation.8 | convolution fusion | flops 43384832 | bytes 8028161 | tf_op jit(solution)/shard_map/lck,lkp->lcp/dot_general | solution.py:283
  (9 shorter events, 0.1 us)
Async XLA Ops:
  6.5 29.4 %copy-start = (s32[128,6]{0,1:T(8,128)S(1)}, s32[128,6]{0,1:T(8,128)}, u32[]{:S(2)}) copy-start(s32[128,6]{0,1:T(8,128)} %param.19) | copy-start | bytes 9220
  6.5 105.8 %all-gather.2.cloned.1.call-start = ((), (), s32[]{:S(2)}) async-start(), calls=%async_computation | async-start | bytes 5013504 | tf_op jit(solution)/shard_map/all_gather | solution.py:205
  7.3 3.3 %copy-start.3 = (pred[128,256]{1,0:T(8,128)(4,1)}, pred[128,256]{1,0:T(8,128)(4,1)S(1)}, u32[]{:S(2)}) copy-start(pred[128,256]{1,0:T(8,128)(4,1)S(1)} %iota_compare_fusion) | copy-start | bytes 98308
  20.6 3.7 %copy-start.1 = (bf16[128,8,256]{2,1,0:T(8,128)(2,1)S(1)}, bf16[128,8,256]{2,1,0:T(8,128)(2,1)}, u32[]{:S(2)}) copy-start(bf16[128,8,256]{2,1,0:T(8,128)(2,1)} %param.12) | copy-start | bytes 1572868
  24.3 6.4 %collective-permute-start = (bf16[4,16,256]{2,1,0:T(8,128)(2,1)S(1)}, bf16[4,16,256]{2,1,0:T(8,128)(2,1)S(1)}, u32[]{:S(2)}, u32[]{:S(2)}) collective-permute-start(bf16[4,16,256]{2,1,0:T(8,128)(2,1)S(1)} %get-tuple-element.13), channel_id=1, source_target_pairs={{0,2},{2,4},{4,6},{6,8},{8,10},{10,12},{12,14},{14,16},{16,18},{18... | collective-permute-start | bytes 98312 | tf_op jit(solution)/shard_map/ppermute | solution.py:177
  29.1 5.8 %collective-permute-start.1 = (bf16[4,16,256]{2,1,0:T(8,128)(2,1)S(1)}, bf16[4,16,256]{2,1,0:T(8,128)(2,1)S(1)}, u32[]{:S(2)}, u32[]{:S(2)}) collective-permute-start(bf16[4,16,256]{2,1,0:T(8,128)(2,1)S(1)} %get-tuple-element.14), channel_id=1, source_target_pairs={{2,0},{4,2},{6,4},{8,6},{10,8},{12,10},{14,12},{16,14},{18,16},{20... | collective-permute-start | bytes 98312 | tf_op jit(solution)/shard_map/ppermute | solution.py:179
  35.9 2.0 %collective-permute-start.2 = (bf16[136,8,256]{2,1,0:T(8,128)(2,1)S(1)}, bf16[136,8,256]{2,1,0:T(8,128)(2,1)S(1)}, u32[]{:S(2)}, u32[]{:S(2)}) collective-permute-start(bf16[136,8,256]{2,1,0:T(8,128)(2,1)S(1)} %get-tuple-element.9), channel_id=1, source_target_pairs={{0,1},{1,0},{2,3},{3,2},{4,5},{5,4},{6,7},{7,6},{8,9},{9,8},{10,11... | collective-permute-start | bytes 1671176 | tf_op jit(solution)/shard_map/ppermute | solution.py:184
  111.7 3.5 %copy-start.7 = (s32[128,8]{0,1:T(8,128)S(1)}, s32[128,8]{0,1:T(8,128)}, u32[]{:S(2)}) copy-start(s32[128,8]{0,1:T(8,128)} %param.20) | copy-start | bytes 12292
  111.7 3.5 %copy-start.8 = (s32[64,8]{0,1:T(8,128)S(1)}, s32[64,8]{0,1:T(8,128)}, u32[]{:S(2)}) copy-start(s32[64,8]{0,1:T(8,128)} %param.22) | copy-start | bytes 6148
  111.7 4.8 %copy-start.5 = (s32[128,8]{0,1:T(8,128)S(1)}, s32[128,8]{0,1:T(8,128)}, u32[]{:S(2)}) copy-start(s32[128,8]{0,1:T(8,128)} %param.21) | copy-start | bytes 12292
  111.7 4.8 %copy-start.6 = (s32[64,8]{0,1:T(8,128)S(1)}, s32[64,8]{0,1:T(8,128)}, u32[]{:S(2)}) copy-start(s32[64,8]{0,1:T(8,128)} %param.23) | copy-start | bytes 6148
  115.1 12.6 %copy-start.2 = (bf16[64,8,64]{2,1,0:T(8,128)(2,1)S(1)}, bf16[64,8,64]{2,1,0:T(8,128)(2,1)}, u32[]{:S(2)}) copy-start(bf16[64,8,64]{2,1,0:T(8,128)(2,1)} %param.18) | copy-start | bytes 196612
  115.1 15.4 %collective-permute-start.3 = (bf16[16,48,8,128]{3,2,1,0:T(8,128)(2,1)}, bf16[16,48,8,128]{3,2,1,0:T(8,128)(2,1)}, u32[]{:S(2)}, u32[]{:S(2)}) collective-permute-start(bf16[16,48,8,128]{3,2,1,0:T(8,128)(2,1)} %slice_select_fusion), channel_id=1, source_target_pairs={{0,1},{1,0},{2,3},{3,2},{4,5},{5,4},{6,7},{7,6},{8,9},{9,8},{10,11... | collective-permute-start | bytes 4718600 | tf_op jit(solution)/shard_map/ppermute | solution.py:229
  118.6 46.0 %collective-permute-start.4 = (f32[64,8,256]{2,1,0:T(8,128)}, f32[64,8,256]{2,1,0:T(8,128)S(1)}, u32[]{:S(2)}, u32[]{:S(2)}) collective-permute-start(f32[64,8,256]{2,1,0:T(8,128)} %get-tuple-element.12), channel_id=1, source_target_pairs={{0,1},{1,0},{2,3},{3,2},{4,5},{5,4},{6,7},{7,6},{8,9},{9,8},{10,11... | collective-permute-start | bytes 1572872 | tf_op jit(solution)/shard_map/ppermute | solution.py:231
  150.2 14.5 %copy-start.4 = (pred[128,256]{1,0:T(8,128)(4,1)S(1)}, pred[128,256]{1,0:T(8,128)(4,1)}, u32[]{:S(2)}) copy-start(pred[128,256]{1,0:T(8,128)(4,1)} %copy-done.3) | copy-start | bytes 98308
Sparse Core Ops, SparseCore 0:
  24.4 83.3 all-gather.1
